TPU v7x, 32 devices: a whole 2x2x4 slice. The times are simulated.
32 devices in a mesh: seq: 8 (over z, x), heads: 4 (over y, core).
Axes of the slice: x: 2, y: 2, z: 4, core: 2. Of those that a mesh axis runs over, the one named last changes fastest.
Arguments:
- query_rows: bfloat16 [4096, 2048], P('seq', 'heads'), may hold values from -8 to 8
- key_rows: bfloat16 [4096, 2048], P('seq', 'heads'), may hold values from -8 to 8
- value_rows: bfloat16 [4096, 2048], P('seq', 'heads'), may hold values from -6 to 6
- doc_ids: int32 [4096], P('seq'), may hold values from 0 to 3, never falling along the last dimension, each value on 1 to 2048 neighbouring positions
- grad_out: bfloat16 [4096, 2048], P('seq', 'heads'), may hold values from -6 to 6
- out_weight: bfloat16 [2048, 2048], P('heads'), may hold values from -0.125 to 0.125
Outputs:
- grad_query: bfloat16 [4096, 2048], P('seq', 'heads')
- grad_keys: bfloat16 [4096, 2048], P('seq', 'heads')
- grad_values: bfloat16 [4096, 2048], P('seq', 'heads')
- grad_weight: float32 [2048, 2048], P('heads', 'seq')
Inputs may be any that keep to these rules, and one draw needn't show every extreme that they name: `doc_ids`: Non-decreasing along the sequence; each document holds at most (2048) tokens.
All inputs are finite; a program needn't handle non-finite values.
Results may differ from a plain program's by a relative error of at most 0.02.
Values may be sent and summed in bfloat16 or wider, within the bound.
A program may use at most 256 MiB of HBM per device.

v0:
```python
import jax
import jax.numpy as jnp
from jax import lax
from jax.sharding import PartitionSpec as P

HD = 64


score_scale = 0.125
very_low = -1e30


def shifted(value, axis, by):
    devices = lax.axis_size(axis)
    pairs = [(i, i + by) for i in range(devices) if 0 <= i + by < devices]
    return lax.ppermute(value, axis, pairs)


def per_head(matrix):
    return matrix.reshape(matrix.shape[0], matrix.shape[1] // HD, HD)


def merged(tensor):
    return jnp.transpose(tensor, (1, 0, 2)).reshape(
        tensor.shape[1], tensor.shape[0] * tensor.shape[2]
    )


def pair_scores(query_part, key_part, query_pos, key_pos, query_doc, key_doc):
    scores = (
        jnp.einsum(
            "qhd,khd->hqk",
            per_head(query_part),
            per_head(key_part),
            preferred_element_type=jnp.float32,
        )
        * score_scale
    )
    allowed = (key_pos[None, :] <= query_pos[:, None]) & (key_doc[None, :] == query_doc[:, None])
    return (scores, allowed[None])


def shards(query_rows, key_rows, value_rows, doc_ids, grad_out, out_weight):
    shard_rows = query_rows.shape[0]
    inner_cols = query_rows.shape[1]
    head_count = inner_cols // HD
    seq_count = lax.axis_size("seq")
    total_rows = shard_rows * seq_count
    first_row = lax.axis_index("seq") * shard_rows
    query_pos = first_row + jnp.arange(shard_rows, dtype=jnp.int32)
    all_docs = lax.all_gather(doc_ids, "seq", axis=0, tiled=True)

    def key_info(offset, length):
        key_pos = offset + jnp.arange(length, dtype=jnp.int32)
        inside = (key_pos >= 0) & (key_pos < total_rows)
        key_doc = lax.dynamic_slice_in_dim(all_docs, offset, length, 0)
        key_doc = jnp.where(inside, key_doc, -1)
        return (key_pos, key_doc)

    init_fwd = (
        jnp.full((head_count, shard_rows), very_low, jnp.float32),
        jnp.zeros((head_count, shard_rows), jnp.float32),
        jnp.zeros((head_count, shard_rows, HD), jnp.float32),
    )
    reach = min(4, seq_count - 1)
    near_keys = []
    near_keys.append((0, key_rows, value_rows))
    for distance in range(1, reach + 1):
        key_in, value_in = shifted((key_rows, value_rows), "seq", distance)
        near_keys.append((distance, key_in, value_in))
    running = init_fwd
    for distance, key_part, value_part in near_keys:
        forward_key_pos, forward_key_doc = key_info(
            first_row - distance * shard_rows, key_part.shape[0]
        )
        forward_run_max, forward_run_sum, forward_run_acc = running
        forward_scores, forward_allowed = pair_scores(
            query_rows, key_part, query_pos, forward_key_pos, doc_ids, forward_key_doc
        )
        forward_scores = jnp.where(forward_allowed, forward_scores, very_low)
        new_max = jnp.maximum(forward_run_max, jnp.max(forward_scores, axis=2))
        forward_attn_prob = jnp.where(
            forward_allowed, jnp.exp(forward_scores - new_max[:, :, None]), 0.0
        )
        factor = jnp.exp(forward_run_max - new_max)
        forward_run_sum = forward_run_sum * factor + jnp.sum(forward_attn_prob, axis=2)
        forward_run_acc = forward_run_acc * factor[:, :, None] + jnp.einsum(
            "hqk,khd->hqd",
            forward_attn_prob.astype(jnp.bfloat16),
            per_head(value_part),
            preferred_element_type=jnp.float32,
        )
        running = (new_max, forward_run_sum, forward_run_acc)
    run_max, run_sum, run_acc = running
    context = merged(run_acc / run_sum[:, :, None]).astype(jnp.bfloat16)
    log_total = run_max + jnp.log(run_sum)
    full_grad = lax.all_gather(grad_out, "heads", axis=1, tiled=True)
    grad_context = lax.dot_general(
        full_grad, out_weight, (((1,), (1,)), ((), ())), preferred_element_type=jnp.float32
    ).astype(jnp.bfloat16)
    weight_term = lax.dot_general(
        context, full_grad, (((0,), (0,)), ((), ())), preferred_element_type=jnp.float32
    )
    grad_weight = lax.psum_scatter(
        weight_term.astype(jnp.bfloat16), "seq", scatter_dimension=1, tiled=True
    ).astype(jnp.float32)
    row_delta = jnp.transpose(
        jnp.sum(
            per_head(grad_context).astype(jnp.float32) * per_head(context).astype(jnp.float32),
            axis=2,
        )
    )

    def owner_core(totals, query_part, grad_part, part_total, part_delta, offset):
        piece_rows = query_part.shape[0]
        piece_pos, piece_doc = key_info(offset, piece_rows)
        key_grad, value_grad = totals
        scores, allowed = pair_scores(
            query_part, key_rows, piece_pos, query_pos, piece_doc, doc_ids
        )
        attn_prob = jnp.where(allowed, jnp.exp(scores - part_total[:, :, None]), 0.0)
        grad_prob = jnp.einsum(
            "qhd,khd->hqk",
            per_head(grad_part),
            per_head(value_rows),
            preferred_element_type=jnp.float32,
        )
        grad_score = attn_prob * (grad_prob - part_delta[:, :, None])
        key_grad = key_grad + jnp.einsum(
            "hqk,qhd->hkd",
            grad_score.astype(jnp.bfloat16),
            per_head(query_part),
            preferred_element_type=jnp.float32,
        )
        value_grad = value_grad + jnp.einsum(
            "hqk,qhd->hkd",
            attn_prob.astype(jnp.bfloat16),
            per_head(grad_part),
            preferred_element_type=jnp.float32,
        )
        return (key_grad, value_grad)

    init_grad = jnp.zeros((head_count, shard_rows, HD), jnp.float32)
    query_acc = init_grad
    for distance, key_part, value_part in near_keys:
        query_key_pos, query_key_doc = key_info(
            first_row - distance * shard_rows, key_part.shape[0]
        )
        query_scores, query_allowed = pair_scores(
            query_rows, key_part, query_pos, query_key_pos, doc_ids, query_key_doc
        )
        query_attn_prob = jnp.where(
            query_allowed, jnp.exp(query_scores - log_total[:, :, None]), 0.0
        )
        query_grad_prob = jnp.einsum(
            "qhd,khd->hqk",
            per_head(grad_context),
            per_head(value_part),
            preferred_element_type=jnp.float32,
        )
        query_grad_score = query_attn_prob * (query_grad_prob - row_delta[:, :, None])
        query_acc = query_acc + jnp.einsum(
            "hqk,khd->hqd",
            query_grad_score.astype(jnp.bfloat16),
            per_head(key_part),
            preferred_element_type=jnp.float32,
        )
    owner_totals = owner_core(
        (init_grad, init_grad), query_rows, grad_context, log_total, row_delta, first_row
    )
    for distance in range(1, reach + 1):
        query_in, grad_in = shifted((query_rows, grad_context), "seq", -distance)
        total_in, delta_in = shifted((log_total, row_delta), "seq", -distance)
        owner_totals = owner_core(
            owner_totals, query_in, grad_in, total_in, delta_in, first_row + distance * shard_rows
        )
    key_acc, value_acc = owner_totals
    grad_keys = (merged(key_acc) * score_scale).astype(jnp.bfloat16)
    grad_values = merged(value_acc).astype(jnp.bfloat16)
    grad_query = (merged(query_acc) * score_scale).astype(jnp.bfloat16)
    return (grad_query, grad_keys, grad_values, grad_weight)


def solution(mesh):
    return jax.shard_map(
        shards,
        mesh=mesh,
        in_specs=(
            P("seq", "heads"),
            P("seq", "heads"),
            P("seq", "heads"),
            P("seq"),
            P("seq", "heads"),
            P("heads", None),
        ),
        out_specs=(P("seq", "heads"), P("seq", "heads"), P("seq", "heads"), P("heads", "seq")),
        check_vma=False,
    )
```

profile of v0, /device:TPU:0, one launch (start us, length us, event | category | flops | bytes accessed | tf_op | source)
XLA Modules:
  0.0 471.8 jit_solution(3108356003628676970)
XLA Ops:
  7.2 6.9 %collective-permute-start.3 = (bf16[512,512]{1,0:T(8,128)(2,1)}, bf16[512,512]{1,0:T(8,128)(2,1)}, u32[]{:S(2)}, u32[]{:S(2)}) collective-permute-start(bf16[512,512]{1,0:T(8,128)(2,1)} %param.7), channel_id=1, source_target_pairs={{0,16},{4,20},{8,24},{12,28},{1,17},{5,21},{9,25},{13,29},{2,18},{... | collective-permute-start | bytes 1572872 | tf_op jit(solution)/shard_map/ppermute | solution.py:16
  14.1 5.2 %collective-permute-start.2 = (bf16[512,512]{1,0:T(8,128)(2,1)}, bf16[512,512]{1,0:T(8,128)(2,1)}, u32[]{:S(2)}, u32[]{:S(2)}) collective-permute-start(bf16[512,512]{1,0:T(8,128)(2,1)} %param.7), channel_id=1, source_target_pairs={{0,12},{4,16},{8,20},{12,24},{16,28},{1,13},{5,17},{9,21},{13,25},... | collective-permute-start | bytes 1572872 | tf_op jit(solution)/shard_map/ppermute | solution.py:16
  19.3 2.1 collective-permute-start.1
  21.4 3.1 collective-permute-start
  24.6 2.1 collective-permute-start.7
  26.8 97.9 %all-gather = s32[8,1,512]{2,1,0:T(1,128)S(1)} all-gather(s32[1,1,512]{2,1,0:T(1,128)} %bitcast.290), channel_id=1, replica_groups=mesh['seq'=8,'heads'=4] {'seq'}, dimensions={0}, use_global_device_ids=true | all-gather | bytes 18432 | tf_op jit(solution)/shard_map/all_gather | solution.py:51
  124.8 4.3 compare_and_fusion.4
  131.7 4.8 %select_reduce_fusion.4 = (f32[8,512]{1,0:T(8,128)S(1)}, f32[8,512,512]{1,2,0:T(8,128)}) fusion(pred[512,512]{0,1:T(8,128)(4,1)S(1)} %get-tuple-element.46, bf16[512,8,64]{0,2,1:T(8,128)(2,1)S(1)} %bitcast.230, bf16[512,8,64]{0,2,1:T(8,128)(2,1)S(1)} %bitcast.236), kind=kOutput, calls=%fused_computation.25 | convolution fusion | flops 274722816 | bytes 9715712 | tf_op jit(solution)/shard_map/qhd,khd->hqk/dot_general | solution.py:31
  136.5 2.1 copy.113
  138.5 2.1 collective-permute-start.6
  140.6 2.0 copy.112
  142.7 5.8 %select_reduce_fusion = (f32[8,512]{1,0:T(8,128)S(1)}, f32[8,512,512]{1,2,0:T(8,128)}) fusion(pred[512,512]{0,1:T(8,128)(4,1)} %get-tuple-element.45, bf16[512,8,64]{0,2,1:T(8,128)(2,1)S(1)} %bitcast.231, bf16[512,8,64]{0,2,1:T(8,128)(2,1)} %bitcast.260), kind=kOutput, calls=%fused_computation.21 | convolution fusion | flops 274722816 | bytes 9715712 | tf_op jit(solution)/shard_map/qhd,khd->hqk/dot_general | solution.py:31
  148.5 3.0 collective-permute-start.5
  151.5 2.0 copy.111
  153.5 5.9 %select_reduce_fusion.1 = (f32[8,512]{1,0:T(8,128)S(1)}, f32[8,512,512]{1,2,0:T(8,128)}) fusion(pred[512,512]{0,1:T(8,128)(4,1)} %get-tuple-element.44, bf16[512,8,64]{0,2,1:T(8,128)(2,1)S(1)} %bitcast.232, bf16[512,8,64]{0,2,1:T(8,128)(2,1)} %bitcast.262), kind=kOutput, calls=%fused_computation.22 | convolution fusion | flops 274722816 | bytes 9715712 | tf_op jit(solution)/shard_map/qhd,khd->hqk/dot_general | solution.py:31
  160.7 2.0 copy.110
  162.8 5.9 %select_reduce_fusion.2 = (f32[8,512]{1,0:T(8,128)S(1)}, f32[8,512,512]{1,2,0:T(8,128)}) fusion(pred[512,512]{0,1:T(8,128)(4,1)} %get-tuple-element.43, bf16[512,8,64]{0,2,1:T(8,128)(2,1)S(1)} %bitcast.233, bf16[512,8,64]{0,2,1:T(8,128)(2,1)} %bitcast.258), kind=kOutput, calls=%fused_computation.23 | convolution fusion | flops 274722816 | bytes 9715712 | tf_op jit(solution)/shard_map/qhd,khd->hqk/dot_general | solution.py:31
  170.2 2.1 copy.109
  172.2 2.7 select_reduce_fusion.3
  175.1 8.1 %fusion.13 = f32[8,512]{1,0:T(8,128)} fusion(f32[8,512,512]{1,2,0:T(8,128)} %get-tuple-element.49, f32[8,512]{1,0:T(8,128)S(1)} %get-tuple-element.20, pred[512,512]{0,1:T(8,128)(4,1)S(1)} %copy-done.12), kind=kLoop, calls=%fused_computation.39 | loop fusion | flops 10481664 | bytes 8683520 | tf_op jit(solution)/shard_map/reduce_sum | solution.py:86
  183.2 2.6 fusion.11
  185.9 2.6 fusion.9
  188.5 2.6 fusion.7
  191.2 2.6 fusion.5
  195.1 2.1 copy.146
  197.1 5.7 %fusion.211 = f32[8,512,512]{1,2,0:T(8,128)} fusion(bf16[512,8,64]{0,2,1:T(8,128)(2,1)} %bitcast.254, bf16[512,8,64]{0,2,1:T(8,128)(2,1)S(1)} %bitcast.237), kind=kOutput, calls=%fused_computation.225 | convolution fusion | flops 268435456 | bytes 9437184 | tf_op jit(solution)/shard_map/qhd,khd->hqk/dot_general | solution.py:31
  202.8 6.1 %collective-permute-start.4 = (bf16[512,512]{1,0:T(8,128)(2,1)}, bf16[512,512]{1,0:T(8,128)(2,1)}, u32[]{:S(2)}, u32[]{:S(2)}) collective-permute-start(bf16[512,512]{1,0:T(8,128)(2,1)} %param.8), channel_id=1, source_target_pairs={{0,4},{4,8},{8,12},{12,16},{16,20},{20,24},{24,28},{1,5},{5,9},{9,... | collective-permute-start | bytes 1572872 | tf_op jit(solution)/shard_map/ppermute | solution.py:16
  209.0 2.1 copy.142
  211.0 5.6 %fusion.210 = f32[8,512,512]{1,2,0:T(8,128)} fusion(bf16[512,8,64]{0,2,1:T(8,128)(2,1)} %bitcast.252, bf16[512,8,64]{0,2,1:T(8,128)(2,1)S(1)} %bitcast.238), kind=kOutput, calls=%fused_computation.224 | convolution fusion | flops 268435456 | bytes 9437184 | tf_op jit(solution)/shard_map/qhd,khd->hqk/dot_general | solution.py:31
  217.9 2.1 copy.134
  220.0 5.6 %fusion.208 = f32[8,512,512]{1,2,0:T(8,128)} fusion(bf16[512,8,64]{0,2,1:T(8,128)(2,1)} %bitcast.264, bf16[512,8,64]{0,2,1:T(8,128)(2,1)S(1)} %bitcast.239), kind=kOutput, calls=%fused_computation.222 | convolution fusion | flops 268435456 | bytes 9437184 | tf_op jit(solution)/shard_map/qhd,khd->hqk/dot_general | solution.py:31
  227.8 2.1 copy.121
  231.1 2.0 copy.119
  234.9 2.0 copy.117
  237.0 2.1 copy.138
  239.1 5.7 %fusion.209 = f32[8,512,512]{1,2,0:T(8,128)} fusion(bf16[512,8,64]{0,2,1:T(8,128)(2,1)} %bitcast.256, bf16[512,8,64]{0,2,1:T(8,128)(2,1)S(1)} %bitcast.240), kind=kOutput, calls=%fused_computation.223 | convolution fusion | flops 268435456 | bytes 9437184 | tf_op jit(solution)/shard_map/qhd,khd->hqk/dot_general | solution.py:31
  244.7 2.1 copy.115
  248.3 6.8 %fusion.91 = f32[512,8,64]{0,2,1:T(8,128)} fusion(bf16[512,8,64]{0,2,1:T(8,128)(2,1)} %bitcast.270, f32[8,512,512]{1,2,0:T(8,128)} %get-tuple-element.49, f32[8,512]{1,0:T(8,128)} %copy-done.36, pred[512,512]{0,1:T(8,128)(4,1)} %get-tuple-element.45), kind=kOutput, calls=%fused_computation.93 | convolution fusion | flops 278921216 | bytes 10240000 | tf_op jit(solution)/shard_map/hqk,khd->hqd/dot_general | solution.py:87
  255.1 6.9 %fusion.88 = f32[512,8,64]{0,2,1:T(8,128)} fusion(bf16[512,8,64]{0,2,1:T(8,128)(2,1)S(1)} %bitcast.273, f32[8,512,512]{1,2,0:T(8,128)} %get-tuple-element.51, f32[8,512]{1,0:T(8,128)S(1)} %get-tuple-element.21, pred[512,512]{0,1:T(8,128)(4,1)S(1)} %copy-done.10), kind=kOutput, calls=%fused_computation.92 | convolution fusion | flops 278921216 | bytes 10240000 | tf_op jit(solution)/shard_map/hqk,khd->hqd/dot_general | solution.py:87
  262.1 3.3 fusion.85
  266.0 3.3 fusion.112
  269.4 3.7 convolution_convert_fusion.1
  273.1 8.6 %multiply_reduce_fusion = (f32[512,8]{0,1:T(8,128)S(1)}, bf16[512,8,64]{0,2,1:T(8,128)(2,1)}) fusion(bf16[512,512]{0,1:T(8,128)(2,1)} %convolution_convert_fusion.1, f32[512,8]{0,1:T(8,128)S(1)} %copy-done.39, f32[512,8,64]{0,2,1:T(8,128)} %fusion.91, f32[512,8]{0,1:T(8,128)S(1)} %copy-done.42, f32[512,8,64]{0,2,1:T(8,128)} %fusion.88, ...), kind=kOutput, calls=%fused_computation.123 | convolution fusion | flops 282324992 | bytes 14516224 | tf_op jit(solution)/shard_map/hqk,khd->hqd/dot_general | solution.py:87
  281.8 8.1 %fusion.37 = f32[8,512,64]{1,2,0:T(8,128)} fusion(bf16[512,8,64]{0,2,1:T(8,128)(2,1)S(1)} %bitcast.261, f32[8,512,512]{1,2,0:T(8,128)} %get-tuple-element.49, f32[8,512]{1,0:T(8,128)S(1)} %bitcast.280, f32[8,512]{1,0:T(8,128)S(1)} %log_add_fusion, pred[512,512]{0,1:T(8,128)(4,1)S(1)} %copy-done.13, bf16[512,8,64]{0,2,1:T(8,128)(2,1)} %bitcast.8, ...), kind=kOutput, calls=%fused_computation.54 | convolution fusion | flops 549453824 | bytes 11304960 | tf_op jit(solution)/shard_map/hqk,khd->hqd/dot_general | solution.py:162
  289.9 8.3 %fusion.36 = f32[8,512,64]{1,2,0:T(8,128)} fusion(bf16[512,8,64]{0,2,1:T(8,128)(2,1)S(1)} %bitcast.263, f32[8,512,512]{1,2,0:T(8,128)} %get-tuple-element.51, f32[8,512]{1,0:T(8,128)S(1)} %bitcast.281, f32[8,512]{1,0:T(8,128)S(1)} %log_add_fusion, pred[512,512]{0,1:T(8,128)(4,1)S(1)} %copy-done.11, bf16[512,8,64]{0,2,1:T(8,128)(2,1)} %bitcast.8, ...), kind=kOutput, calls=%fused_computation.53 | convolution fusion | flops 549453824 | bytes 11304960 | tf_op jit(solution)/shard_map/hqk,khd->hqd/dot_general | solution.py:162
  298.2 2.3 fusion.207
  303.8 7.4 %fusion.33 = f32[8,512,64]{1,2,0:T(8,128)} fusion(bf16[512,8,64]{0,2,1:T(8,128)(2,1)S(1)} %bitcast.241, f32[8,512,512]{1,2,0:T(8,128)S(1)} %fusion.207, f32[8,512,512]{1,2,0:T(8,128)} %get-tuple-element.57, f32[8,512]{1,0:T(8,128)S(1)} %bitcast.283, f32[8,512]{1,0:T(8,128)S(1)} %log_add_fusion, pred[512,512]{0,1:T(8,128)(4,1)S(1)} %get-tuple-element.46), kind=kOutput, calls=%fused_computation.50 | convolution fusion | flops 281018368 | bytes 18644992 | tf_op jit(solution)/shard_map/hqk,khd->hqd/dot_general | solution.py:162
  311.1 8.3 %fusion.142 = f32[8,512,64]{1,2,0:T(8,128)} fusion(f32[8,512,64]{1,2,0:T(8,128)} %fusion.33, bf16[512,8,64]{0,2,1:T(8,128)(2,1)S(1)} %bitcast.267, f32[8,512,512]{1,2,0:T(8,128)} %copy-done.3, f32[8,512]{1,0:T(8,128)S(1)} %bitcast.284, f32[8,512]{1,0:T(8,128)S(1)} %log_add_fusion, pred[512,512]{0,1:T(8,128)(4,1)S(1)} %copy-done.8, ...), kind=kOutput, calls=%fused_computation.116 | convolution fusion | flops 549715968 | bytes 12353536 | tf_op jit(solution)/shard_map/hqk,khd->hqd/dot_general | solution.py:162
  319.5 8.7 %fusion.38 = f32[8,512,64]{1,2,0:T(8,128)} fusion(bf16[512,8,64]{0,2,1:T(8,128)(2,1)S(1)} %bitcast.235, f32[8,512,512]{1,2,0:T(8,128)} %copy-done.2, f32[8,512,512]{1,2,0:T(8,128)} %get-tuple-element.57, f32[8,512]{1,0:T(8,128)S(1)} %bitcast.285, f32[8,512]{1,0:T(8,128)S(1)} %log_add_fusion, pred[512,512]{0,1:T(8,128)(4,1)S(1)} %copy-done.24), kind=kOutput, calls=%fused_computation.55 | convolution fusion | flops 281018368 | bytes 18644992 | tf_op jit(solution)/shard_map/hqk,qhd->hkd/dot_general | solution.py:129
  328.2 8.8 %fusion.143 = bf16[8,512,64]{1,2,0:T(8,128)(2,1)} fusion(f32[8,512,64]{1,2,0:T(8,128)} %fusion.37, f32[8,512,64]{1,2,0:T(8,128)} %fusion.36, f32[8,512,64]{1,2,0:T(8,128)} %fusion.142, bf16[512,8,64]{0,2,1:T(8,128)(2,1)S(1)} %bitcast.259, f32[8,512,512]{1,2,0:T(8,128)} %get-tuple-element.53, f32[8,512]{1,0:T(8,128)S(1)} %bitcast.286, ...), kind=kOutput, calls=%fused_computation.119 | convolution fusion | flops 550764544 | bytes 13926400 | tf_op jit(solution)/shard_map/hqk,khd->hqd/dot_general | solution.py:162
  337.0 6.3 %fusion.22 = f32[8,512,64]{1,2,0:T(8,128)} fusion(bf16[512,8,64]{0,2,1:T(8,128)(2,1)} %bitcast.8, f32[8,512,512]{1,2,0:T(8,128)} %get-tuple-element.57, f32[8,512]{1,0:T(8,128)S(1)} %log_add_fusion, pred[512,512]{0,1:T(8,128)(4,1)S(1)} %copy-done.24), kind=kOutput, calls=%fused_computation.44 | convolution fusion | flops 276824064 | bytes 10240000 | tf_op jit(solution)/shard_map/hqk,qhd->hkd/dot_general | solution.py:135
  343.3 2.6 convolution_convert_fusion
  350.9 8.3 %fusion.137 = f32[8,512,64]{1,2,0:T(8,128)} fusion(f32[8,512,64]{1,2,0:T(8,128)S(1)} %copy-done.25, bf16[512,8,64]{0,2,1:T(8,128)(2,1)S(1)} %bitcast.265, f32[8,512,512]{1,2,0:T(8,128)} %fusion.208, f32[8,512]{1,0:T(8,128)S(1)} %collective-permute-done.11, f32[8,512]{1,0:T(8,128)} %collective-permute-done.9, pred[512,512]{0,1:T(8,128)(4,1)S(1)} %copy-done.32, ...), kind=kOutput, calls=%fused_computation.111 | convolution fusion | flops 549715968 | bytes 12353536 | tf_op jit(solution)/shard_map/hqk,qhd->hkd/dot_general | solution.py:129
  360.5 9.7 %collective-permute-done.23 = f32[8,512]{1,0:T(8,128)S(1)} collective-permute-done((f32[8,512]{1,0:T(8,128)S(1)}, f32[8,512]{1,0:T(8,128)S(1)}, u32[]{:S(2)}, u32[]{:S(2)}) %collective-permute-start.23) | collective-permute-done | bytes 16416 | tf_op jit(solution)/shard_map/ppermute | solution.py:16
  371.5 39.8 %collective-permute-done.22 = bf16[512,512]{0,1:T(8,128)(2,1)} collective-permute-done((bf16[512,512]{0,1:T(8,128)(2,1)}, bf16[512,512]{0,1:T(8,128)(2,1)}, u32[]{:S(2)}, u32[]{:S(2)}) %collective-permute-start.22) | collective-permute-done | bytes 524320 | tf_op jit(solution)/shard_map/ppermute | solution.py:16
  412.6 8.3 %fusion.42 = f32[8,512,64]{1,2,0:T(8,128)} fusion(bf16[512,8,64]{0,2,1:T(8,128)(2,1)S(1)} %bitcast.255, f32[8,512,512]{1,2,0:T(8,128)} %fusion.211, f32[8,512]{1,0:T(8,128)S(1)} %collective-permute-done.23, f32[8,512]{1,0:T(8,128)} %collective-permute-done.21, pred[512,512]{0,1:T(8,128)(4,1)S(1)} %copy-done.35, bf16[512,8,64]{0,2,1:T(8,128)(2,1)} %bitcast.39, ...), kind=kOutput, calls=%fused_computation.59 | convolution fusion | flops 549453824 | bytes 11304960 | tf_op jit(solution)/shard_map/hqk,qhd->hkd/dot_general | solution.py:129
  422.4 8.3 %fusion.41 = f32[8,512,64]{1,2,0:T(8,128)} fusion(bf16[512,8,64]{0,2,1:T(8,128)(2,1)S(1)} %bitcast.253, f32[8,512,512]{1,2,0:T(8,128)} %fusion.210, f32[8,512]{1,0:T(8,128)S(1)} %collective-permute-done.19, f32[8,512]{1,0:T(8,128)} %collective-permute-done.17, pred[512,512]{0,1:T(8,128)(4,1)S(1)} %copy-done.34, bf16[512,8,64]{0,2,1:T(8,128)(2,1)S(1)} %bitcast.291, ...), kind=kOutput, calls=%fused_computation.58 | convolution fusion | flops 549453824 | bytes 11304960 | tf_op jit(solution)/shard_map/hqk,qhd->hkd/dot_general | solution.py:129
  430.7 2.5 collective-permute-done.14
  433.2 8.3 %fusion.144 = bf16[8,512,64]{1,2,0:T(8,128)(2,1)S(1)} fusion(f32[8,512,64]{1,2,0:T(8,128)} %fusion.42, f32[8,512,64]{1,2,0:T(8,128)} %fusion.41, f32[8,512,64]{1,2,0:T(8,128)} %fusion.137, bf16[512,8,64]{0,2,1:T(8,128)(2,1)S(1)} %bitcast.257, f32[8,512,512]{1,2,0:T(8,128)} %fusion.209, f32[8,512]{1,0:T(8,128)S(1)} %collective-permute-done.15, ...), kind=kOutput, calls=%fused_computation.120 | convolution fusion | flops 550764544 | bytes 13926400 | tf_op jit(solution)/shard_map/hqk,qhd->hkd/dot_general | solution.py:129
  442.6 5.3 %fusion.14 = f32[8,512,64]{1,2,0:T(8,128)S(1)} fusion(bf16[512,8,64]{0,2,1:T(8,128)(2,1)} %bitcast.39, f32[8,512,512]{1,2,0:T(8,128)} %fusion.211, f32[8,512]{1,0:T(8,128)} %collective-permute-done.21, pred[512,512]{0,1:T(8,128)(4,1)S(1)} %copy-done.35), kind=kOutput, calls=%fused_computation.40 | convolution fusion | flops 276824064 | bytes 10240000 | tf_op jit(solution)/shard_map/hqk,qhd->hkd/dot_general | solution.py:135
  447.9 6.3 %fusion.16 = f32[8,512,64]{1,2,0:T(8,128)} fusion(bf16[512,8,64]{0,2,1:T(8,128)(2,1)S(1)} %bitcast.292, f32[8,512,512]{1,2,0:T(8,128)} %fusion.210, f32[8,512]{1,0:T(8,128)} %collective-permute-done.17, pred[512,512]{0,1:T(8,128)(4,1)S(1)} %copy-done.34), kind=kOutput, calls=%fused_computation.41 | convolution fusion | flops 276824064 | bytes 10240000 | tf_op jit(solution)/shard_map/hqk,qhd->hkd/dot_general | solution.py:135
  454.2 4.0 fusion.18
  458.2 3.7 fusion.145
  463.0 1.8 convert_element_type.129
  (183 shorter events, 31.1 us)
Async XLA Ops:
  7.2 262.2 %copy-start = (bf16[512,2048]{1,0:T(8,128)(2,1)S(1)}, bf16[512,2048]{1,0:T(8,128)(2,1)}, u32[]{:S(2)}) copy-start(bf16[512,2048]{1,0:T(8,128)(2,1)} %param.11) | copy-start | bytes 6291460
  7.2 262.2 %all-gather.3.cloned.1.call-start = ((), (), s32[]{:S(2)}) async-start(), calls=%async_computation.1 | async-start | bytes 2621440 | tf_op jit(solution)/shard_map/all_gather | solution.py:97
  7.2 131.3 %collective-permute-start.3 = (bf16[512,512]{1,0:T(8,128)(2,1)}, bf16[512,512]{1,0:T(8,128)(2,1)}, u32[]{:S(2)}, u32[]{:S(2)}) collective-permute-start(bf16[512,512]{1,0:T(8,128)(2,1)} %param.7), channel_id=1, source_target_pairs={{0,16},{4,20},{8,24},{12,28},{1,17},{5,21},{9,25},{13,29},{2,18},{... | collective-permute-start | bytes 1572872 | tf_op jit(solution)/shard_map/ppermute | solution.py:16
  14.1 134.4 %collective-permute-start.2 = (bf16[512,512]{1,0:T(8,128)(2,1)}, bf16[512,512]{1,0:T(8,128)(2,1)}, u32[]{:S(2)}, u32[]{:S(2)}) collective-permute-start(bf16[512,512]{1,0:T(8,128)(2,1)} %param.7), channel_id=1, source_target_pairs={{0,12},{4,16},{8,20},{12,24},{16,28},{1,13},{5,17},{9,21},{13,25},... | collective-permute-start | bytes 1572872 | tf_op jit(solution)/shard_map/ppermute | solution.py:16
  19.3 140.1 %collective-permute-start.1 = (bf16[512,512]{1,0:T(8,128)(2,1)}, bf16[512,512]{1,0:T(8,128)(2,1)}, u32[]{:S(2)}, u32[]{:S(2)}) collective-permute-start(bf16[512,512]{1,0:T(8,128)(2,1)} %param.7), channel_id=1, source_target_pairs={{0,8},{4,12},{8,16},{12,20},{16,24},{20,28},{1,9},{5,13},{9,17},{1... | collective-permute-start | bytes 1572872 | tf_op jit(solution)/shard_map/ppermute | solution.py:16
  21.4 147.2 %collective-permute-start = (bf16[512,512]{1,0:T(8,128)(2,1)}, bf16[512,512]{1,0:T(8,128)(2,1)}, u32[]{:S(2)}, u32[]{:S(2)}) collective-permute-start(bf16[512,512]{1,0:T(8,128)(2,1)} %param.7), channel_id=1, source_target_pairs={{0,4},{4,8},{8,12},{12,16},{16,20},{20,24},{24,28},{1,5},{5,9},{9,... | collective-permute-start | bytes 1572872 | tf_op jit(solution)/shard_map/ppermute | solution.py:16
  24.6 438.4 %reduce-scatter.2.cloned.1.call-start = ((), (), s32[]{:S(2)}) async-start(), calls=%async_computation.2 | async-start | bytes 2359296 | tf_op jit(solution)/shard_map/reduce_scatter | solution.py:104
  24.6 201.8 %collective-permute-start.7 = (bf16[512,512]{1,0:T(8,128)(2,1)}, bf16[512,512]{1,0:T(8,128)(2,1)}, u32[]{:S(2)}, u32[]{:S(2)}) collective-permute-start(bf16[512,512]{1,0:T(8,128)(2,1)} %param.8), channel_id=1, source_target_pairs={{0,16},{4,20},{8,24},{12,28},{1,17},{5,21},{9,25},{13,29},{2,18},{... | collective-permute-start | bytes 1572872 | tf_op jit(solution)/shard_map/ppermute | solution.py:16
  138.5 91.3 %collective-permute-start.6 = (bf16[512,512]{1,0:T(8,128)(2,1)}, bf16[512,512]{1,0:T(8,128)(2,1)}, u32[]{:S(2)}, u32[]{:S(2)}) collective-permute-start(bf16[512,512]{1,0:T(8,128)(2,1)} %param.8), channel_id=1, source_target_pairs={{0,12},{4,16},{8,20},{12,24},{16,28},{1,13},{5,17},{9,21},{13,25},... | collective-permute-start | bytes 1572872 | tf_op jit(solution)/shard_map/ppermute | solution.py:16
  148.5 84.7 %collective-permute-start.5 = (bf16[512,512]{1,0:T(8,128)(2,1)}, bf16[512,512]{1,0:T(8,128)(2,1)}, u32[]{:S(2)}, u32[]{:S(2)}) collective-permute-start(bf16[512,512]{1,0:T(8,128)(2,1)} %param.8), channel_id=1, source_target_pairs={{0,8},{4,12},{8,16},{12,20},{16,24},{20,28},{1,9},{5,13},{9,17},{1... | collective-permute-start | bytes 1572872 | tf_op jit(solution)/shard_map/ppermute | solution.py:16
  159.4 34.4 %collective-permute-start.20 = (bf16[512,512]{1,0:T(8,128)(2,1)}, bf16[512,512]{1,0:T(8,128)(2,1)}, u32[]{:S(2)}, u32[]{:S(2)}) collective-permute-start(bf16[512,512]{1,0:T(8,128)(2,1)} %param.6), channel_id=1, source_target_pairs={{16,0},{20,4},{24,8},{28,12},{17,1},{21,5},{25,9},{29,13},{18,2},{... | collective-permute-start | bytes 1572872 | tf_op jit(solution)/shard_map/ppermute | solution.py:16
  168.6 34.2 %collective-permute-start.16 = (bf16[512,512]{1,0:T(8,128)(2,1)}, bf16[512,512]{1,0:T(8,128)(2,1)}, u32[]{:S(2)}, u32[]{:S(2)}) collective-permute-start(bf16[512,512]{1,0:T(8,128)(2,1)} %param.6), channel_id=1, source_target_pairs={{12,0},{16,4},{20,8},{24,12},{28,16},{13,1},{17,5},{21,9},{25,13},... | collective-permute-start | bytes 1572872 | tf_op jit(solution)/shard_map/ppermute | solution.py:16
  172.2 11.0 %slice-start.8 = ((s8[8388608]{0:T(1024)(128)(4,1)}), s8[4194304]{0:T(1024)(128)(4,1)S(1)}, s32[]{:S(2)}) async-start(s8[8388608]{0:T(1024)(128)(4,1)} %bitcast.228), calls=%async_computation.11 | async-start | bytes 8388608
  172.2 11.0 %slice-start.9 = ((s8[8388608]{0:T(1024)(128)(4,1)}), s8[4194304]{0:T(1024)(128)(4,1)S(1)}, s32[]{:S(2)}) async-start(s8[8388608]{0:T(1024)(128)(4,1)} %bitcast.228), calls=%async_computation.12 | async-start | bytes 8388608
  172.2 11.0 %copy-start.9 = (pred[512,512]{0,1:T(8,128)(4,1)S(1)}, pred[512,512]{0,1:T(8,128)(4,1)}, u32[]{:S(2)}) copy-start(pred[512,512]{0,1:T(8,128)(4,1)} %get-tuple-element.44) | copy-start | bytes 786436
  175.0 13.5 %copy-start.3 = (f32[8,512,512]{1,2,0:T(8,128)}, f32[8,512,512]{1,2,0:T(8,128)S(1)}, u32[]{:S(2)}) copy-start(f32[8,512,512]{1,2,0:T(8,128)S(1)} %get-tuple-element.55) | copy-start | bytes 25165828
  175.0 10.8 %copy-start.36 = (f32[8,512]{1,0:T(8,128)}, f32[8,512]{1,0:T(8,128)S(1)}, u32[]{:S(2)}) copy-start(f32[8,512]{1,0:T(8,128)S(1)} %get-tuple-element.20) | copy-start | bytes 49156
  175.0 16.1 %copy-start.37 = (f32[8,512]{1,0:T(8,128)}, f32[8,512]{1,0:T(8,128)S(1)}, u32[]{:S(2)}) copy-start(f32[8,512]{1,0:T(8,128)S(1)} %get-tuple-element.35) | copy-start | bytes 49156
  175.0 10.8 %slice-start.4 = ((s8[8388608]{0:T(1024)(128)(4,1)}), s8[4194304]{0:T(1024)(128)(4,1)S(1)}, s32[]{:S(2)}) async-start(s8[8388608]{0:T(1024)(128)(4,1)} %bitcast.224), calls=%async_computation.7 | async-start | bytes 8388608
  175.1 10.8 %copy-start.4 = (pred[512,512]{0,1:T(8,128)(4,1)S(1)}, pred[512,512]{0,1:T(8,128)(4,1)}, u32[]{:S(2)}) copy-start(pred[512,512]{0,1:T(8,128)(4,1)} %get-tuple-element.43) | copy-start | bytes 786436
  193.8 22.9 %collective-permute-start.8 = (bf16[512,512]{1,0:T(8,128)(2,1)}, bf16[512,512]{1,0:T(8,128)(2,1)}, u32[]{:S(2)}, u32[]{:S(2)}) collective-permute-start(bf16[512,512]{1,0:T(8,128)(2,1)} %param.6), channel_id=1, source_target_pairs={{4,0},{8,4},{12,8},{16,12},{20,16},{24,20},{28,24},{5,1},{9,5},{13... | collective-permute-start | bytes 1572872 | tf_op jit(solution)/shard_map/ppermute | solution.py:16
  202.8 41.9 %collective-permute-start.4 = (bf16[512,512]{1,0:T(8,128)(2,1)}, bf16[512,512]{1,0:T(8,128)(2,1)}, u32[]{:S(2)}, u32[]{:S(2)}) collective-permute-start(bf16[512,512]{1,0:T(8,128)(2,1)} %param.8), channel_id=1, source_target_pairs={{0,4},{4,8},{8,12},{12,16},{16,20},{20,24},{24,28},{1,5},{5,9},{9,... | collective-permute-start | bytes 1572872 | tf_op jit(solution)/shard_map/ppermute | solution.py:16
  216.7 20.3 %collective-permute-start.12 = (bf16[512,512]{1,0:T(8,128)(2,1)}, bf16[512,512]{1,0:T(8,128)(2,1)}, u32[]{:S(2)}, u32[]{:S(2)}) collective-permute-start(bf16[512,512]{1,0:T(8,128)(2,1)} %param.6), channel_id=1, source_target_pairs={{8,0},{12,4},{16,8},{20,12},{24,16},{28,20},{9,1},{13,5},{17,9},{2... | collective-permute-start | bytes 1572872 | tf_op jit(solution)/shard_map/ppermute | solution.py:16
  226.5 132.7 %collective-permute-start.21 = (f32[8,512]{1,0:T(8,128)S(1)}, f32[8,512]{1,0:T(8,128)}, u32[]{:S(2)}, u32[]{:S(2)}) collective-permute-start(f32[8,512]{1,0:T(8,128)S(1)} %log_add_fusion), channel_id=1, source_target_pairs={{16,0},{20,4},{24,8},{28,12},{17,1},{21,5},{25,9},{29,13},{18,2},{... | collective-permute-start | bytes 49160 | tf_op jit(solution)/shard_map/ppermute | solution.py:16
  229.8 191.0 %collective-permute-start.17 = (f32[8,512]{1,0:T(8,128)S(1)}, f32[8,512]{1,0:T(8,128)}, u32[]{:S(2)}, u32[]{:S(2)}) collective-permute-start(f32[8,512]{1,0:T(8,128)S(1)} %log_add_fusion), channel_id=1, source_target_pairs={{12,0},{16,4},{20,8},{24,12},{28,16},{13,1},{17,5},{21,9},{25,13},... | collective-permute-start | bytes 49160 | tf_op jit(solution)/shard_map/ppermute | solution.py:16
  233.2 113.7 %collective-permute-start.9 = (f32[8,512]{1,0:T(8,128)S(1)}, f32[8,512]{1,0:T(8,128)}, u32[]{:S(2)}, u32[]{:S(2)}) collective-permute-start(f32[8,512]{1,0:T(8,128)S(1)} %log_add_fusion), channel_id=1, source_target_pairs={{4,0},{8,4},{12,8},{16,12},{20,16},{24,20},{28,24},{5,1},{9,5},{13... | collective-permute-start | bytes 49160 | tf_op jit(solution)/shard_map/ppermute | solution.py:16
  246.8 8.3 %copy-start.10 = (pred[512,512]{0,1:T(8,128)(4,1)S(1)}, pred[512,512]{0,1:T(8,128)(4,1)}, u32[]{:S(2)}) copy-start(pred[512,512]{0,1:T(8,128)(4,1)} %get-tuple-element.44) | copy-start | bytes 786436
  246.8 8.3 %copy-start.29 = (bf16[512,512]{0,1:T(8,128)(2,1)S(1)}, bf16[512,512]{0,1:T(8,128)(2,1)}, u32[]{:S(2)}) copy-start(bf16[512,512]{0,1:T(8,128)(2,1)} %copy.119) | copy-start | bytes 1572868
  266.0 7.0 %copy-start.42 = (f32[512,8]{0,1:T(8,128)S(1)}, f32[512,8]{0,1:T(8,128)}, u32[]{:S(2)}) copy-start(f32[512,8]{0,1:T(8,128)} %get-tuple-element.19) | copy-start | bytes 49156
  273.1 8.7 %copy-start.13 = (pred[512,512]{0,1:T(8,128)(4,1)S(1)}, pred[512,512]{0,1:T(8,128)(4,1)}, u32[]{:S(2)}) copy-start(pred[512,512]{0,1:T(8,128)(4,1)} %get-tuple-element.45) | copy-start | bytes 786436
  273.1 8.7 %copy-start.20 = (bf16[512,512]{0,1:T(8,128)(2,1)S(1)}, bf16[512,512]{0,1:T(8,128)(2,1)}, u32[]{:S(2)}) copy-start(bf16[512,512]{0,1:T(8,128)(2,1)} %copy.112) | copy-start | bytes 1572868
  273.1 8.7 %copy-start.28 = (bf16[512,512]{0,1:T(8,128)(2,1)S(1)}, bf16[512,512]{0,1:T(8,128)(2,1)}, u32[]{:S(2)}) copy-start(bf16[512,512]{0,1:T(8,128)(2,1)} %copy.121) | copy-start | bytes 1572868
  281.8 8.1 %copy-start.11 = (pred[512,512]{0,1:T(8,128)(4,1)S(1)}, pred[512,512]{0,1:T(8,128)(4,1)}, u32[]{:S(2)}) copy-start(pred[512,512]{0,1:T(8,128)(4,1)} %get-tuple-element.44) | copy-start | bytes 786436
  281.8 8.1 %copy-start.21 = (bf16[512,512]{0,1:T(8,128)(2,1)S(1)}, bf16[512,512]{0,1:T(8,128)(2,1)}, u32[]{:S(2)}) copy-start(bf16[512,512]{0,1:T(8,128)(2,1)} %copy.111) | copy-start | bytes 1572868
  289.9 8.3 %copy-start.15 = (bf16[512,512]{0,1:T(8,128)(2,1)S(1)}, bf16[512,512]{0,1:T(8,128)(2,1)}, u32[]{:S(2)}) copy-start(bf16[512,512]{0,1:T(8,128)(2,1)} %copy.113) | copy-start | bytes 1572868
  300.5 10.6 %copy-start.8 = (pred[512,512]{0,1:T(8,128)(4,1)S(1)}, pred[512,512]{0,1:T(8,128)(4,1)}, u32[]{:S(2)}) copy-start(pred[512,512]{0,1:T(8,128)(4,1)} %get-tuple-element.42) | copy-start | bytes 786436
  300.5 10.6 %copy-start.23 = (bf16[512,512]{0,1:T(8,128)(2,1)S(1)}, bf16[512,512]{0,1:T(8,128)(2,1)}, u32[]{:S(2)}) copy-start(bf16[512,512]{0,1:T(8,128)(2,1)} %copy.109) | copy-start | bytes 1572868
  300.5 10.6 %copy-start.30 = (bf16[512,512]{0,1:T(8,128)(2,1)S(1)}, bf16[512,512]{0,1:T(8,128)(2,1)}, u32[]{:S(2)}) copy-start(bf16[512,512]{0,1:T(8,128)(2,1)} %copy.115) | copy-start | bytes 1572868
  300.6 47.6 %collective-permute-start.11 = (f32[8,512]{1,0:T(8,128)S(1)}, f32[8,512]{1,0:T(8,128)S(1)}, u32[]{:S(2)}, u32[]{:S(2)}) collective-permute-start(f32[8,512]{1,0:T(8,128)S(1)} %bitcast.282), channel_id=1, source_target_pairs={{4,0},{8,4},{12,8},{16,12},{20,16},{24,20},{28,24},{5,1},{9,5},{13... | collective-permute-start | bytes 49160 | tf_op jit(solution)/shard_map/ppermute | solution.py:16
  302.1 47.4 %collective-permute-start.10 = (bf16[512,512]{0,1:T(8,128)(2,1)}, bf16[512,512]{0,1:T(8,128)(2,1)}, u32[]{:S(2)}, u32[]{:S(2)}) collective-permute-start(bf16[512,512]{0,1:T(8,128)(2,1)} %convolution_convert_fusion.1), channel_id=1, source_target_pairs={{4,0},{8,4},{12,8},{16,12},{20,16},{24,20},{28,24},{5,1},{9,5},{13... | collective-permute-start | bytes 1572872 | tf_op jit(solution)/shard_map/ppermute | solution.py:16
  311.1 8.3 %copy-start.24 = (pred[512,512]{0,1:T(8,128)(4,1)S(1)}, pred[512,512]{0,1:T(8,128)(4,1)}, u32[]{:S(2)}) copy-start(pred[512,512]{0,1:T(8,128)(4,1)} %get-tuple-element.47) | copy-start | bytes 786436
  319.4 8.7 %copy-start.6 = (pred[512,512]{0,1:T(8,128)(4,1)S(1)}, pred[512,512]{0,1:T(8,128)(4,1)}, u32[]{:S(2)}) copy-start(pred[512,512]{0,1:T(8,128)(4,1)} %get-tuple-element.43) | copy-start | bytes 786436
  319.4 8.7 %copy-start.19 = (bf16[512,512]{0,1:T(8,128)(2,1)S(1)}, bf16[512,512]{0,1:T(8,128)(2,1)}, u32[]{:S(2)}) copy-start(bf16[512,512]{0,1:T(8,128)(2,1)} %copy.110) | copy-start | bytes 1572868
  319.4 8.7 %copy-start.27 = (bf16[512,512]{0,1:T(8,128)(2,1)S(1)}, bf16[512,512]{0,1:T(8,128)(2,1)}, u32[]{:S(2)}) copy-start(bf16[512,512]{0,1:T(8,128)(2,1)} %copy.117) | copy-start | bytes 1572868
  337.0 8.9 %copy-start.31 = (bf16[8,512,64]{1,2,0:T(8,128)(2,1)S(1)}, bf16[8,512,64]{1,2,0:T(8,128)(2,1)}, u32[]{:S(2)}) copy-start(bf16[8,512,64]{1,2,0:T(8,128)(2,1)} %fusion.143) | copy-start | bytes 1572868
  343.3 7.6 %copy-start.22 = (bf16[512,512]{0,1:T(8,128)(2,1)S(1)}, bf16[512,512]{0,1:T(8,128)(2,1)}, u32[]{:S(2)}) copy-start(bf16[512,512]{0,1:T(8,128)(2,1)} %copy.134) | copy-start | bytes 1572868
  343.3 7.6 %copy-start.25 = (f32[8,512,64]{1,2,0:T(8,128)S(1)}, f32[8,512,64]{1,2,0:T(8,128)}, u32[]{:S(2)}) copy-start(f32[8,512,64]{1,2,0:T(8,128)} %fusion.38) | copy-start | bytes 3145732
  343.3 7.6 %copy-start.32 = (pred[512,512]{0,1:T(8,128)(4,1)S(1)}, pred[512,512]{0,1:T(8,128)(4,1)}, u32[]{:S(2)}) copy-start(pred[512,512]{0,1:T(8,128)(4,1)} %get-tuple-element.39) | copy-start | bytes 786436
  346.9 83.8 %collective-permute-start.13 = (f32[8,512]{1,0:T(8,128)S(1)}, f32[8,512]{1,0:T(8,128)S(1)}, u32[]{:S(2)}, u32[]{:S(2)}) collective-permute-start(f32[8,512]{1,0:T(8,128)S(1)} %log_add_fusion), channel_id=1, source_target_pairs={{8,0},{12,4},{16,8},{20,12},{24,16},{28,20},{9,1},{13,5},{17,9},{2... | collective-permute-start | bytes 49160 | tf_op jit(solution)/shard_map/ppermute | solution.py:16
  348.2 22.0 %collective-permute-start.23 = (f32[8,512]{1,0:T(8,128)S(1)}, f32[8,512]{1,0:T(8,128)S(1)}, u32[]{:S(2)}, u32[]{:S(2)}) collective-permute-start(f32[8,512]{1,0:T(8,128)S(1)} %bitcast.287), channel_id=1, source_target_pairs={{16,0},{20,4},{24,8},{28,12},{17,1},{21,5},{25,9},{29,13},{18,2},{... | collective-permute-start | bytes 49160 | tf_op jit(solution)/shard_map/ppermute | solution.py:16
  349.5 61.7 %collective-permute-start.22 = (bf16[512,512]{0,1:T(8,128)(2,1)}, bf16[512,512]{0,1:T(8,128)(2,1)}, u32[]{:S(2)}, u32[]{:S(2)}) collective-permute-start(bf16[512,512]{0,1:T(8,128)(2,1)} %convolution_convert_fusion.1), channel_id=1, source_target_pairs={{16,0},{20,4},{24,8},{28,12},{17,1},{21,5},{25,9},{29,13},{18,2},{... | collective-permute-start | bytes 1572872 | tf_op jit(solution)/shard_map/ppermute | solution.py:16
  350.9 61.7 %copy-start.17 = (bf16[512,512]{0,1:T(8,128)(2,1)S(1)}, bf16[512,512]{0,1:T(8,128)(2,1)}, u32[]{:S(2)}) copy-start(bf16[512,512]{0,1:T(8,128)(2,1)} %copy.146) | copy-start | bytes 1572868
  350.9 61.7 %copy-start.35 = (pred[512,512]{0,1:T(8,128)(4,1)S(1)}, pred[512,512]{0,1:T(8,128)(4,1)}, u32[]{:S(2)}) copy-start(pred[512,512]{0,1:T(8,128)(4,1)} %get-tuple-element.41) | copy-start | bytes 786436
  359.2 63.2 %collective-permute-start.19 = (f32[8,512]{1,0:T(8,128)S(1)}, f32[8,512]{1,0:T(8,128)S(1)}, u32[]{:S(2)}, u32[]{:S(2)}) collective-permute-start(f32[8,512]{1,0:T(8,128)S(1)} %bitcast.288), channel_id=1, source_target_pairs={{12,0},{16,4},{20,8},{24,12},{28,16},{13,1},{17,5},{21,9},{25,13},... | collective-permute-start | bytes 49160 | tf_op jit(solution)/shard_map/ppermute | solution.py:16
  370.2 52.1 %collective-permute-start.18 = (bf16[512,512]{0,1:T(8,128)(2,1)}, bf16[512,512]{0,1:T(8,128)(2,1)S(1)}, u32[]{:S(2)}, u32[]{:S(2)}) collective-permute-start(bf16[512,512]{0,1:T(8,128)(2,1)} %convolution_convert_fusion.1), channel_id=1, source_target_pairs={{12,0},{16,4},{20,8},{24,12},{28,16},{13,1},{17,5},{21,9},{25,13},... | collective-permute-start | bytes 1572872 | tf_op jit(solution)/shard_map/ppermute | solution.py:16
  411.3 19.5 %collective-permute-start.15 = (f32[8,512]{1,0:T(8,128)S(1)}, f32[8,512]{1,0:T(8,128)S(1)}, u32[]{:S(2)}, u32[]{:S(2)}) collective-permute-start(f32[8,512]{1,0:T(8,128)S(1)} %bitcast.289), channel_id=1, source_target_pairs={{8,0},{12,4},{16,8},{20,12},{24,16},{28,20},{9,1},{13,5},{17,9},{2... | collective-permute-start | bytes 49160 | tf_op jit(solution)/shard_map/ppermute | solution.py:16
  412.6 9.8 %copy-start.16 = (bf16[512,512]{0,1:T(8,128)(2,1)S(1)}, bf16[512,512]{0,1:T(8,128)(2,1)}, u32[]{:S(2)}) copy-start(bf16[512,512]{0,1:T(8,128)(2,1)} %copy.142) | copy-start | bytes 1572868
  412.6 9.8 %copy-start.34 = (pred[512,512]{0,1:T(8,128)(4,1)S(1)}, pred[512,512]{0,1:T(8,128)(4,1)}, u32[]{:S(2)}) copy-start(pred[512,512]{0,1:T(8,128)(4,1)} %get-tuple-element.40) | copy-start | bytes 786436
  420.9 12.4 %collective-permute-start.14 = (bf16[512,512]{0,1:T(8,128)(2,1)}, bf16[512,512]{0,1:T(8,128)(2,1)}, u32[]{:S(2)}, u32[]{:S(2)}) collective-permute-start(bf16[512,512]{0,1:T(8,128)(2,1)} %convolution_convert_fusion.1), channel_id=1, source_target_pairs={{8,0},{12,4},{16,8},{20,12},{24,16},{28,20},{9,1},{13,5},{17,9},{2... | collective-permute-start | bytes 1572872 | tf_op jit(solution)/shard_map/ppermute | solution.py:16
  422.4 10.9 %copy-start.18 = (bf16[512,512]{0,1:T(8,128)(2,1)S(1)}, bf16[512,512]{0,1:T(8,128)(2,1)}, u32[]{:S(2)}) copy-start(bf16[512,512]{0,1:T(8,128)(2,1)} %copy.138) | copy-start | bytes 1572868
  422.4 10.9 %copy-start.33 = (pred[512,512]{0,1:T(8,128)(4,1)S(1)}, pred[512,512]{0,1:T(8,128)(4,1)}, u32[]{:S(2)}) copy-start(pred[512,512]{0,1:T(8,128)(4,1)} %get-tuple-element.38) | copy-start | bytes 786436
  442.5 11.7 %slice-start.12 = ((s8[8388608]{0:T(1024)(128)(4,1)}), s8[4194304]{0:T(1024)(128)(4,1)S(1)}, s32[]{:S(2)}) async-start(s8[8388608]{0:T(1024)(128)(4,1)} %bitcast.244), calls=%async_computation.15 | async-start | bytes 8388608
  447.9 10.3 %slice-start.10 = ((s8[8388608]{0:T(1024)(128)(4,1)}), s8[4194304]{0:T(1024)(128)(4,1)S(1)}, s32[]{:S(2)}) async-start(s8[8388608]{0:T(1024)(128)(4,1)} %bitcast.242), calls=%async_computation.13 | async-start | bytes 8388608
  454.2 10.5 %copy-start.1 = (bf16[512,2048]{1,0:T(8,128)(2,1)S(1)}, bf16[512,2048]{1,0:T(8,128)(2,1)}, u32[]{:S(2)}) copy-start(bf16[512,2048]{1,0:T(8,128)(2,1)} %param.11) | copy-start | bytes 6291460
  (22 other events, 111.7 us)
Sparse Core Ops, SparseCore 0:
  24.7 19.8 all-gather.2
  347.0 108.8 reduce-scatter.1
where the time goes:
time: 480 us; the launch traced here: 472 us
  matrix products  194 us (40%)
  blocking collectives  97.9 us (20%)
  starting transfers between devices  52.4 us (11%)
  waiting for transfers between devices  52.1 us (11%)
  local copies, waits for them, and re-layouts  33.5 us (7%)
  other arithmetic  27.2 us (6%)
  between operations  15 us (3%)
    all_gather x1, blocking collectives, shards(): all_docs = lax.all_gather(doc_ids, 'seq', axis=0, tiled=True)  97.9 us
    ppermute x24, starting transfers between devices, shifted(): return lax.ppermute(value, axis, pairs)  52.3 us
    ppermute x24, waiting for transfers between devices, shifted(): return lax.ppermute(value, axis, pairs)  52.1 us
    dot_general x9, matrix products, pair_scores(): jnp.einsum('qhd,khd->hqk', per_head(query_part), per_head(key_part), pref...  47.8 us
    dot_general x5, matrix products, owner_core(): jnp.einsum('hqk,qhd->hkd', grad_score.astype(jnp.bfloat16), per_head(quer...  41.9 us
    dot_general x5, matrix products, shards(): jnp.einsum('hqk,khd->hqd', query_grad_score.astype(jnp.bfloat16), per_hea...  40.9 us
    dot_general x5, matrix products, shards(): jnp.einsum('hqk,khd->hqd', forward_attn_prob.astype(jnp.bfloat16), per_he...  29 us
    dot_general x5, matrix products, owner_core(): jnp.einsum('hqk,qhd->hkd', attn_prob.astype(jnp.bfloat16), per_head(grad_...  25.6 us
  transfers between devices with their start and end apart: 26, of which 3 were waited for; matrix products, arithmetic and copies ran while one was open for 53% of the time, Pallas kernels for 0%

commit v1 on v0

--- a/solution.py
+++ b/solution.py
@@ -1,6 +1,11 @@
+import functools
+import math
+
 import jax
 import jax.numpy as jnp
 from jax import lax
+from jax.experimental import pallas as pl
+from jax.experimental.pallas import tpu as pltpu
 from jax.sharding import PartitionSpec as P
 
 HD = 64
@@ -40,7 +45,415 @@
     return (scores, allowed[None])
 
 
-def shards(query_rows, key_rows, value_rows, doc_ids, grad_out, out_weight):
+BLOCK = 512
+LOG2E = math.log2(math.e)
+EXP2_SCALE = score_scale * LOG2E
+MESH = pl.DeviceIdType.MESH
+VMEM = pl.BlockSpec(memory_space=pltpu.VMEM)
+SMEM = pl.BlockSpec(memory_space=pltpu.SMEM)
+HBM = pl.BlockSpec(memory_space=pl.ANY)
+
+
+def mod(a, b):
+    return lax.rem(a, jnp.int32(b))
+
+
+def div(a, b):
+    return lax.div(a, jnp.int32(b))
+
+
+def greet(count, heads):
+    me = lax.axis_index("seq")
+    mine = lax.axis_index("heads")
+    barrier = pltpu.get_barrier_semaphore()
+    for step in range(1, count):
+        pl.semaphore_signal(
+            barrier, inc=1, device_id={"seq": mod(me + step, count)}, device_id_type=MESH
+        )
+    for step in range(1, heads):
+        pl.semaphore_signal(
+            barrier, inc=1, device_id={"heads": mod(mine + step, heads)}, device_id_type=MESH
+        )
+    pl.semaphore_wait(barrier, count - 1 + heads - 1)
+
+
+def remote(src, dst, send, recv, slot, axis, peer):
+    return pltpu.make_async_remote_copy(
+        src_ref=src,
+        dst_ref=dst,
+        send_sem=send.at[slot],
+        recv_sem=recv.at[slot],
+        device_id={axis: peer},
+        device_id_type=MESH,
+    )
+
+
+def head_rows(owner):
+    return pl.ds(pl.multiple_of(owner * HD, HD), HD)
+
+
+def token_cols(owner, cols):
+    return pl.ds(pl.multiple_of(owner * cols, cols), cols)
+
+
+def gather_kernel(
+    count, heads, x_ref, doc_ref, grad_ref, weight_ref,
+    qkv_ref, all_doc_ref, dctx_ref, full_ref,
+    grads, dctx, xsend, xrecv, dsend, drecv, gsend, grecv, csend, crecv, local,
+):
+    me = lax.axis_index("seq")
+    mine = lax.axis_index("heads")
+    cols = x_ref.shape[2]
+    width = grad_ref.shape[1]
+    greet(count, heads)
+    here = token_cols(me, cols)
+    own = [
+        pltpu.make_async_copy(grad_ref, grads.at[mine], local.at[0]),
+        pltpu.make_async_copy(doc_ref, all_doc_ref.at[me], local.at[1]),
+        pltpu.make_async_copy(x_ref.at[:, head_rows(me), :], qkv_ref.at[:, :, here], local.at[2]),
+    ]
+    for copy in own:
+        copy.start()
+    wide = [
+        remote(grad_ref, grads.at[mine], gsend, grecv, step, "heads", mod(mine + step, heads))
+        for step in range(1, heads)
+    ]
+    peers = [mod(me + step, count) for step in range(1, count)]
+    rest = [
+        remote(doc_ref, all_doc_ref.at[me], dsend, drecv, step, "seq", peer)
+        for step, peer in enumerate(peers)
+    ] + [
+        remote(
+            x_ref.at[:, head_rows(peer), :], qkv_ref.at[:, :, here], xsend, xrecv, step, "seq", peer
+        )
+        for step, peer in enumerate(peers)
+    ]
+    for copy in wide + rest:
+        copy.start()
+    own[0].wait()
+    for copy in wide:
+        copy.wait()
+    keep = pltpu.make_async_copy(grads, full_ref, local.at[0])
+    keep.start()
+    total = None
+    for part in range(heads):
+        term = nt_dot(weight_ref[:, part * width : (part + 1) * width], grads[part])
+        total = term if total is None else total + term
+    dctx[...] = total.astype(jnp.bfloat16)
+    last = [
+        remote(dctx.at[head_rows(peer), :], dctx_ref.at[0, :, here], csend, crecv, step, "seq", peer)
+        for step, peer in enumerate(peers)
+    ]
+    for copy in last:
+        copy.start()
+    own_dctx = pltpu.make_async_copy(dctx.at[head_rows(me), :], dctx_ref.at[0, :, here], local.at[3])
+    own_dctx.start()
+    for copy in own[1:] + rest + last:
+        copy.wait()
+    own_dctx.wait()
+    keep.wait()
+
+
+def gather(x, docs, grad_out, weight, count, heads):
+    kinds, rows, cols = x.shape
+    docs = docs.reshape(-1, 128)
+    dma = pltpu.SemaphoreType.DMA
+    return pl.pallas_call(
+        functools.partial(gather_kernel, count, heads),
+        out_shape=[
+            jax.ShapeDtypeStruct((kinds, rows // count, cols * count), x.dtype),
+            jax.ShapeDtypeStruct((count,) + docs.shape, docs.dtype),
+            jax.ShapeDtypeStruct((1, rows // count, cols * count), x.dtype),
+            jax.ShapeDtypeStruct((heads,) + grad_out.shape, grad_out.dtype),
+        ],
+        in_specs=[HBM, HBM, HBM, VMEM],
+        out_specs=[HBM] * 4,
+        scratch_shapes=[
+            pltpu.VMEM((heads,) + grad_out.shape, grad_out.dtype),
+            pltpu.VMEM((rows, cols), x.dtype),
+        ]
+        + [dma((count,))] * 4
+        + [dma((heads,))] * 2
+        + [dma((count,))] * 2
+        + [dma((4,))],
+        compiler_params=pltpu.CompilerParams(
+            collective_id=0, has_side_effects=True, vmem_limit_bytes=40 << 20
+        ),
+    )(x, docs, grad_out, weight)
+
+
+def return_kernel(
+    count, x_ref, full_ref, back_ref, out_ref,
+    ctx, own_sum, xout, xin, pout, pin, cout, cin,
+    ksend, krecv, gsend, grecv, xsend, xrecv, psend, precv, csend, crecv, local,
+):
+    me = lax.axis_index("seq")
+    z, x = div(me, 2), mod(me, 2)
+    depth = count // 2
+    cols = x_ref.shape[2] // count
+    half = own_sum.shape[2]
+    greet(count, 1)
+    here = head_rows(me)
+    own_ctx = pltpu.make_async_copy(
+        x_ref.at[3, :, token_cols(me, cols)], ctx.at[here, :], local.at[0]
+    )
+    own_back = pltpu.make_async_copy(
+        x_ref.at[0:3, :, token_cols(me, cols)], back_ref.at[:, here, :], local.at[1]
+    )
+    peers = [mod(me + step, count) for step in range(1, count)]
+    first = [
+        remote(x_ref.at[3, :, token_cols(peer, cols)], ctx.at[here, :], ksend, krecv, step, "seq", peer)
+        for step, peer in enumerate(peers)
+    ]
+    grads = [
+        remote(
+            x_ref.at[0:3, :, token_cols(peer, cols)], back_ref.at[:, here, :],
+            gsend, grecv, step, "seq", peer,
+        )
+        for step, peer in enumerate(peers)
+    ]
+    own_ctx.start()
+    for copy in first + grads:
+        copy.start()
+    own_back.start()
+    own_ctx.wait()
+    for copy in first:
+        copy.wait()
+
+    def product(part, side):
+        at = pl.ds(pl.multiple_of(side * half, half), half)
+        return jnp.dot(ctx[...], full_ref[part, :, at], preferred_element_type=jnp.float32)
+
+    across = []
+    for part in range(depth):
+        xout[part] = product(part, 1 - x).astype(jnp.bfloat16)
+        copy = remote(
+            xout.at[part], xin.at[part], xsend, xrecv, part, "seq", z * 2 + 1 - x
+        )
+        copy.start()
+        across.append(copy)
+    for part in range(depth):
+        own_sum[part] = product(part, x)
+    for part in range(depth):
+        across[part].wait()
+        own_sum[part] += xin[part].astype(jnp.float32)
+    pair = z + 1 - 2 * mod(z, 2)
+    far = mod(z + 2, 4)
+    pair_far = mod(pair + 2, 4)
+    near = []
+    for slot, block in enumerate((pair_far, pair)):
+        pout[slot] = own_sum[block].astype(jnp.bfloat16)
+        copy = remote(pout.at[slot], pin.at[slot], psend, precv, slot, "seq", pair * 2 + x)
+        copy.start()
+        near.append(copy)
+    near[0].wait()
+    cout[...] = (own_sum[far] + pin[0].astype(jnp.float32)).astype(jnp.bfloat16)
+    cross = remote(cout, cin, csend, crecv, 0, "seq", far * 2 + x)
+    cross.start()
+    near[1].wait()
+    cross.wait()
+    out_ref[...] = own_sum[z] + pin[1].astype(jnp.float32) + cin[...].astype(jnp.float32)
+    own_back.wait()
+    for copy in grads:
+        copy.wait()
+
+
+def give_back(x, full, count):
+    kinds, rows, tokens = x.shape
+    inner, cols = rows * count, tokens // count
+    depth = count // 2
+    half = full.shape[2] // 2
+    dma = pltpu.SemaphoreType.DMA
+    bf16 = jnp.bfloat16
+    block = (inner, half)
+    return pl.pallas_call(
+        functools.partial(return_kernel, count),
+        out_shape=[
+            jax.ShapeDtypeStruct((kinds - 1, inner, cols), x.dtype),
+            jax.ShapeDtypeStruct(block, jnp.float32),
+        ],
+        in_specs=[HBM, VMEM],
+        out_specs=[HBM, VMEM],
+        scratch_shapes=[
+            pltpu.VMEM((inner, cols), bf16),
+            pltpu.VMEM((depth,) + block, jnp.float32),
+            pltpu.VMEM((depth,) + block, bf16),
+            pltpu.VMEM((depth,) + block, bf16),
+            pltpu.VMEM((2,) + block, bf16),
+            pltpu.VMEM((2,) + block, bf16),
+            pltpu.VMEM(block, bf16),
+            pltpu.VMEM(block, bf16),
+        ]
+        + [dma((count,))] * 4
+        + [dma((depth,))] * 2
+        + [dma((2,))] * 2
+        + [dma((1,))] * 2
+        + [dma((2,))],
+        compiler_params=pltpu.CompilerParams(
+            collective_id=1, has_side_effects=True, vmem_limit_bytes=40 << 20
+        ),
+    )(x, full)
+
+
+def nt_dot(a, b):
+    return lax.dot_general(a, b, (((1,), (1,)), ((), ())), preferred_element_type=jnp.float32)
+
+
+def block_at(index):
+    return pl.ds(pl.multiple_of(index * BLOCK, BLOCK), BLOCK)
+
+
+def rows_of(cols_ref, slot, rows_ref, blocks):
+    def step(b, _):
+        at = block_at(b)
+        rows_ref[at, :] = cols_ref[slot, :, at].T
+        return 0
+
+    lax.fori_loop(0, blocks, step, 0)
+
+
+def scaled_scores(key_rows, query_cols, first_key, first_query, start, masked):
+    scores = jnp.dot(key_rows, query_cols, preferred_element_type=jnp.float32) * EXP2_SCALE
+    if masked:
+        key_pos = first_key + lax.broadcasted_iota(jnp.int32, scores.shape, 0)
+        query_pos = first_query + lax.broadcasted_iota(jnp.int32, (1, scores.shape[1]), 1)
+        allowed = (key_pos <= query_pos) & (key_pos >= start)
+        scores = jnp.where(allowed, scores, very_low)
+    return scores
+
+
+def attention_kernel(
+    low_ref, full_ref, start_ref, qkv_ref, dctx_ref, out_ref,
+    key_rows, value_rows, key_acc, value_acc,
+):
+    blocks = qkv_ref.shape[2] // BLOCK
+    rows_of(qkv_ref, 1, key_rows, blocks)
+    rows_of(qkv_ref, 2, value_rows, blocks)
+
+    def query_block(j, _):
+        cols = block_at(j)
+        query_cols = qkv_ref[0, :, cols]
+        start = start_ref[:, cols]
+        low, full = low_ref[j], full_ref[j]
+
+        def scores_of(i, masked):
+            return scaled_scores(
+                key_rows[block_at(i), :], query_cols, i * BLOCK, j * BLOCK, start, masked
+            )
+
+        scores = scores_of(j, True)
+        run_max = jnp.max(scores, axis=0, keepdims=True)
+        prob = jnp.exp2(scores - run_max)
+        run_sum = jnp.sum(prob, axis=0, keepdims=True)
+        acc = jnp.dot(
+            qkv_ref[2, :, cols], prob.astype(jnp.bfloat16), preferred_element_type=jnp.float32
+        )
+
+        def forward(masked, i, state):
+            run_max, run_sum, acc = state
+            scores = scores_of(i, masked)
+            new_max = jnp.maximum(run_max, jnp.max(scores, axis=0, keepdims=True))
+            factor = jnp.exp2(run_max - new_max)
+            prob = jnp.exp2(scores - new_max)
+            run_sum = run_sum * factor + jnp.sum(prob, axis=0, keepdims=True)
+            acc = acc * factor + jnp.dot(
+                qkv_ref[2, :, block_at(i)],
+                prob.astype(jnp.bfloat16),
+                preferred_element_type=jnp.float32,
+            )
+            return new_max, run_sum, acc
+
+        state = (run_max, run_sum, acc)
+        state = lax.fori_loop(low, full, functools.partial(forward, True), state)
+        state = lax.fori_loop(full, j, functools.partial(forward, False), state)
+        run_max, run_sum, acc = state
+        context = (acc / run_sum).astype(jnp.bfloat16)
+        out_ref[3, :, cols] = context
+        total = run_max + jnp.log(run_sum) * LOG2E
+        grad_cols = dctx_ref[0, :, cols]
+        delta = jnp.sum(
+            grad_cols.astype(jnp.float32) * context.astype(jnp.float32), axis=0, keepdims=True
+        )
+
+        def backward(i, masked):
+            keys = block_at(i)
+            prob = jnp.exp2(scores_of(i, masked) - total)
+            grad_prob = jnp.dot(
+                value_rows[keys, :], grad_cols, preferred_element_type=jnp.float32
+            )
+            grad_score = (prob * (grad_prob - delta)).astype(jnp.bfloat16)
+            value_term = nt_dot(grad_cols, prob.astype(jnp.bfloat16))
+            key_term = nt_dot(query_cols, grad_score)
+            query_term = jnp.dot(
+                qkv_ref[1, :, keys], grad_score, preferred_element_type=jnp.float32
+            )
+            return keys, key_term, value_term, query_term
+
+        keys, key_term, value_term, query_acc = backward(j, True)
+        key_acc[:, keys] = key_term
+        value_acc[:, keys] = value_term
+
+        def step(masked, i, query_acc):
+            keys, key_term, value_term, query_term = backward(i, masked)
+            key_acc[:, keys] += key_term
+            value_acc[:, keys] += value_term
+            return query_acc + query_term
+
+        query_acc = lax.fori_loop(low, full, functools.partial(step, True), query_acc)
+        query_acc = lax.fori_loop(full, j, functools.partial(step, False), query_acc)
+        out_ref[0, :, cols] = (query_acc * score_scale).astype(jnp.bfloat16)
+        return 0
+
+    lax.fori_loop(0, blocks, query_block, 0)
+
+    def finish(b, _):
+        at = block_at(b)
+        out_ref[1, :, at] = (key_acc[:, at] * score_scale).astype(jnp.bfloat16)
+        out_ref[2, :, at] = value_acc[:, at].astype(jnp.bfloat16)
+        return 0
+
+    lax.fori_loop(0, blocks, finish, 0)
+
+
+def attention(low, full, start, qkv, dctx):
+    tokens = qkv.shape[2]
+    return pl.pallas_call(
+        attention_kernel,
+        out_shape=jax.ShapeDtypeStruct((4, HD, tokens), jnp.bfloat16),
+        in_specs=[SMEM, SMEM, VMEM, VMEM, VMEM],
+        out_specs=VMEM,
+        scratch_shapes=[pltpu.VMEM((tokens, HD), jnp.bfloat16)] * 2
+        + [pltpu.VMEM((HD, tokens), jnp.float32)] * 2,
+        compiler_params=pltpu.CompilerParams(vmem_limit_bytes=40 << 20),
+    )(low, full, start, qkv, dctx)
+
+
+def doc_ranges(docs):
+    tokens = docs.shape[0]
+    ids = jnp.arange(8, dtype=jnp.int32)
+    begins = jnp.sum((docs[None, :] < ids[:, None]).astype(jnp.int32), axis=1)
+    start = jnp.sum(jnp.where(docs[None, :] == ids[:, None], begins[:, None], 0), axis=0)
+    blocks = tokens // BLOCK
+    grouped = start.reshape(blocks, BLOCK)
+    low = grouped[:, 0] // BLOCK
+    full = (grouped[:, BLOCK - 1] + BLOCK - 1) // BLOCK
+    full = jnp.minimum(full, jnp.arange(blocks, dtype=jnp.int32))
+    return low, full, start[None]
+
+
+def head_shards(query_rows, key_rows, value_rows, doc_ids, grad_out, out_weight):
+    count = lax.axis_size("seq")
+    stacked = jnp.stack([query_rows.T, key_rows.T, value_rows.T])
+    qkv, docs, dctx, full_grad = gather(
+        stacked, doc_ids, grad_out, out_weight, count, lax.axis_size("heads")
+    )
+    low, full, start = doc_ranges(docs.reshape(-1))
+    results = attention(low, full, start, qkv, dctx)
+    back, grad_weight = give_back(results, full_grad, count)
+    return (back[0].T, back[1].T, back[2].T, grad_weight)
+
+
+def ring_shards(query_rows, key_rows, value_rows, doc_ids, grad_out, out_weight):
     shard_rows = query_rows.shape[0]
     inner_cols = query_rows.shape[1]
     head_count = inner_cols // HD
@@ -182,6 +595,12 @@
 
 
 def solution(mesh):
+    def shards(query_rows, *others):
+        heads_here = query_rows.shape[1] // HD
+        if heads_here == mesh.shape["seq"] == 2 * mesh.shape["heads"] == 8 and query_rows.shape[0] % BLOCK == 0:
+            return head_shards(query_rows, *others)
+        return ring_shards(query_rows, *others)
+
     return jax.shard_map(
         shards,
         mesh=mesh,

time: 480 us -> 181 us (0.38); the launches traced: 472 us -> 178 us
  matrix products: 194 us -> 0 us
  Pallas kernels: 0 us -> 166 us
  blocking collectives: 97.9 us -> 0 us
  starting transfers between devices: 52.4 us -> 0 us
  waiting for transfers between devices: 52.1 us -> 0 us
  other arithmetic: 27.2 us -> 0.63 us
  local copies, waits for them, and re-layouts: 33.5 us -> 10.7 us
  between operations: 15 us -> 0.76 us
    dot_general x32 -> x0, matrix products: 194 us -> none  [the longest x9 47.8 us: pair_scores(): jnp.einsum('qhd,khd->hqk', per_head(query_part), per_head(key_part), pref...]
    pallas_call x0 -> x3, Pallas kernels: none -> 166 us  [the longest x1 81.8 us: give_back(): pl.pallas_call(functools.partial(return_kernel, count), out_shape=[jax.Sh...]
    all_gather x1 -> x0, blocking collectives: 97.9 us -> none  [shards(): all_docs = lax.all_gather(doc_ids, 'seq', axis=0, tiled=True)]
    ppermute x24 -> x0, starting transfers between devices: 52.3 us -> none  [shifted(): return lax.ppermute(value, axis, pairs)]
    ppermute x24 -> x0, waiting for transfers between devices: 52.1 us -> none  [shifted(): return lax.ppermute(value, axis, pairs)]
    ppermute x12 -> x0, local copies, waits for them, and re-layouts: 24.7 us -> none  [shifted(): return lax.ppermute(value, axis, pairs)]
    reduce_sum x5 -> x2, other arithmetic: 18.6 us -> 0.26 us  [the longest x1 0.15 us: doc_ranges(): begins = jnp.sum((docs[None, :] < ids[:, None]).astype(jnp.int32), axis=1)]
    unnamed x126 -> x19, local copies, waits for them, and re-layouts: 8.81 us -> 10.6 us
  transfers between devices with their start and end apart: 26 -> 0, of which waited for: 3 -> 0; matrix products, arithmetic and copies ran while one was open for 53% -> 0% of each run, Pallas kernels for 0% -> 0%
where the time goes in v1:
time: 181 us; the launch traced here: 178 us
  Pallas kernels  166 us (92%)
  local copies, waits for them, and re-layouts  10.7 us (6%)
    pallas_call x1, Pallas kernels, give_back(): pl.pallas_call(functools.partial(return_kernel, count), out_shape=[jax.Sh...  81.8 us
    pallas_call x1, Pallas kernels, gather(): pl.pallas_call(functools.partial(gather_kernel, count, heads), out_shape=...  49.7 us
    pallas_call x1, Pallas kernels, attention(): pl.pallas_call(attention_kernel, out_shape=jax.ShapeDtypeStruct((4, HD, t...  34.3 us
    unnamed x19, local copies, waits for them, and re-layouts  10.6 us

profile of v1, /device:TPU:0, one launch (start us, length us, event | category | flops | bytes accessed | tf_op | source)
XLA Modules:
  0.0 178.0 jit_solution(6413851251911216241)
XLA Ops:
  0.6 0.0 copy-start.5
  0.6 1.3 copy.28
  2.0 1.3 copy.29
  3.2 0.0 copy-done.5
  3.2 0.2 copy.30
  3.4 0.0 copy-start
  3.5 0.0 copy-start.3
  3.5 0.0 copy-start.4
  3.5 0.2 pad_maximum_fusion.x_ref
  3.7 1.4 copy-done
  5.0 0.1 copy-done.3
  5.1 0.0 copy-done.4
  5.1 49.7 %shard_map.93 = (bf16[3,64,4096]{2,1,0:T(8,128)(2,1)S(1)}, s32[8,4,128]{2,1,0:T(4,128)S(1)}, bf16[1,64,4096]{2,1,0:T(8,128)(2,1)S(1)}, bf16[4,512,512]{2,1,0:T(8,128)(2,1)S(1)}) custom-call(bf16[3,512,512]{2,1,0:T(8,128)(2,1)S(1)} %pad_maximum_fusion.x_ref, s32[4,128]{1,0:T(4,128)S(1)} %bitcast.27, bf16[512,512]{1,0:T(8,128)(2,1)S(1)} %copy-done.3, ...), custom_call_target="tpu_custom_call" | custom-call | tf_op jit(solution)/shard_map/pallas_call | solution.py:161
  54.9 0.0 copy-start.1
  54.9 1.1 copy-done.1
  56.0 0.1 convert_reduce_fusion
  56.2 0.1 select_reduce_fusion
  56.3 0.2 fusion
  56.5 0.0 copy-start.2
  56.5 1.4 copy-done.2
  57.9 34.3 %shard_map.94.x_ref = bf16[4,64,4096]{2,1,0:T(8,128)(2,1)S(1)} custom-call(s32[8]{0:T(128)S(1)} %get-tuple-element.37.low_ref, s32[8]{0:T(128)S(1)} %get-tuple-element.38.full_ref, s32[1,4096]{1,0:T(1,128)S(1)} %bitcast.24, bf16[3,64,4096]{2,1,0:T(8,128)(2,1)S(1)} %copy-done.2, bf16[1,64,4096]{2,1,0:T(8,128)(2,1)S(1)} %get-tuple-element.12.dctx_ref), custom_call_target="tpu_custom_call" | custom-call | tf_op jit(solution)/shard_map/pallas_call | solution.py:420
  92.2 81.8 %shard_map.95 = (bf16[3,512,512]{2,1,0:T(8,128)(2,1)S(1)}, f32[512,256]{1,0:T(8,128)S(1)}) custom-call(bf16[4,64,4096]{2,1,0:T(8,128)(2,1)S(1)} %shard_map.94.x_ref, bf16[4,512,512]{2,1,0:T(8,128)(2,1)S(1)} %get-tuple-element.13.full_ref), custom_call_target="tpu_custom_call" | custom-call | tf_op jit(solution)/shard_map/pallas_call | solution.py:269
  174.1 0.1 slice_bitcast_fusion
  174.2 1.0 copy.33
  175.2 1.0 copy.32
  176.2 1.0 copy.31
  177.2 0.8 copy.35
  (2 shorter events, 0.0 us)
Async XLA Ops:
  0.6 2.6 %copy-start.5 = (bf16[512,512]{1,0:T(8,128)(2,1)S(1)}, bf16[512,512]{1,0:T(8,128)(2,1)}, u32[]{:S(2)}) copy-start(bf16[512,512]{1,0:T(8,128)(2,1)} %param.8) | copy-start | bytes 1572868
  3.4 1.6 copy-start
  3.5 1.7 copy-start.3
  3.5 1.7 copy-start.4
  54.9 1.2 copy-start.1
  56.5 1.4 copy-start.2

commit v2 on v1

--- a/solution.py
+++ b/solution.py
@@ -46,6 +46,7 @@
 
 
 BLOCK = 512
+MAX_DOC = 2048
 LOG2E = math.log2(math.e)
 EXP2_SCALE = score_scale * LOG2E
 MESH = pl.DeviceIdType.MESH
@@ -114,9 +115,12 @@
     ]
     for copy in own:
         copy.start()
+    sibling = mine + 1 - 2 * mod(mine, 2)
+    far = mod(mine + 2, 4)
+    far_sibling = mod(sibling + 2, 4)
     wide = [
-        remote(grad_ref, grads.at[mine], gsend, grecv, step, "heads", mod(mine + step, heads))
-        for step in range(1, heads)
+        remote(grad_ref, grads.at[mine], gsend, grecv, 0, "heads", far),
+        remote(grad_ref, grads.at[mine], gsend, grecv, 1, "heads", sibling),
     ]
     peers = [mod(me + step, count) for step in range(1, count)]
     rest = [
@@ -130,15 +134,21 @@
     ]
     for copy in wide + rest:
         copy.start()
+    def product(part):
+        at = pl.ds(pl.multiple_of(part * width, width), width)
+        return nt_dot(weight_ref[:, at], grads[part])
+
     own[0].wait()
-    for copy in wide:
-        copy.wait()
+    total = product(mine)
+    wide[0].wait()
+    onward = remote(grads.at[far], grads.at[far], gsend, grecv, 2, "heads", sibling)
+    onward.start()
+    wide[1].wait()
+    total = total + product(sibling) + product(far)
+    onward.wait()
     keep = pltpu.make_async_copy(grads, full_ref, local.at[0])
     keep.start()
-    total = None
-    for part in range(heads):
-        term = nt_dot(weight_ref[:, part * width : (part + 1) * width], grads[part])
-        total = term if total is None else total + term
+    total = total + product(far_sibling)
     dctx[...] = total.astype(jnp.bfloat16)
     last = [
         remote(dctx.at[head_rows(peer), :], dctx_ref.at[0, :, here], csend, crecv, step, "seq", peer)
@@ -213,7 +223,7 @@
         for step, peer in enumerate(peers)
     ]
     own_ctx.start()
-    for copy in first + grads:
+    for copy in first:
         copy.start()
     own_back.start()
     own_ctx.wait()
@@ -224,35 +234,38 @@
         at = pl.ds(pl.multiple_of(side * half, half), half)
         return jnp.dot(ctx[...], full_ref[part, :, at], preferred_element_type=jnp.float32)
 
+    pair = z + 1 - 2 * mod(z, 2)
+    far = mod(z + 2, 4)
+    order = (mod(pair + 2, 4), pair, far, z)
     across = []
-    for part in range(depth):
-        xout[part] = product(part, 1 - x).astype(jnp.bfloat16)
-        copy = remote(
-            xout.at[part], xin.at[part], xsend, xrecv, part, "seq", z * 2 + 1 - x
-        )
+    for slot, part in enumerate(order):
+        xout[slot] = product(part, 1 - x).astype(jnp.bfloat16)
+        copy = remote(xout.at[slot], xin.at[slot], xsend, xrecv, slot, "seq", z * 2 + 1 - x)
         copy.start()
         across.append(copy)
-    for part in range(depth):
-        own_sum[part] = product(part, x)
-    for part in range(depth):
-        across[part].wait()
-        own_sum[part] += xin[part].astype(jnp.float32)
-    pair = z + 1 - 2 * mod(z, 2)
-    far = mod(z + 2, 4)
-    pair_far = mod(pair + 2, 4)
+    for copy in grads:
+        copy.start()
+    for slot, part in enumerate(order):
+        own_sum[slot] = product(part, x)
     near = []
-    for slot, block in enumerate((pair_far, pair)):
-        pout[slot] = own_sum[block].astype(jnp.bfloat16)
+    for slot in range(2):
+        across[slot].wait()
+        pout[slot] = (own_sum[slot] + xin[slot].astype(jnp.float32)).astype(jnp.bfloat16)
         copy = remote(pout.at[slot], pin.at[slot], psend, precv, slot, "seq", pair * 2 + x)
         copy.start()
         near.append(copy)
+    across[2].wait()
     near[0].wait()
-    cout[...] = (own_sum[far] + pin[0].astype(jnp.float32)).astype(jnp.bfloat16)
+    cout[...] = (
+        own_sum[2] + xin[2].astype(jnp.float32) + pin[0].astype(jnp.float32)
+    ).astype(jnp.bfloat16)
     cross = remote(cout, cin, csend, crecv, 0, "seq", far * 2 + x)
     cross.start()
+    across[3].wait()
     near[1].wait()
+    own_sum[3] += xin[3].astype(jnp.float32) + pin[1].astype(jnp.float32)
     cross.wait()
-    out_ref[...] = own_sum[z] + pin[1].astype(jnp.float32) + cin[...].astype(jnp.float32)
+    out_ref[...] = own_sum[3] + cin[...].astype(jnp.float32)
     own_back.wait()
     for copy in grads:
         copy.wait()
@@ -312,19 +325,9 @@
     lax.fori_loop(0, blocks, step, 0)
 
 
-def scaled_scores(key_rows, query_cols, first_key, first_query, start, masked):
-    scores = jnp.dot(key_rows, query_cols, preferred_element_type=jnp.float32) * EXP2_SCALE
-    if masked:
-        key_pos = first_key + lax.broadcasted_iota(jnp.int32, scores.shape, 0)
-        query_pos = first_query + lax.broadcasted_iota(jnp.int32, (1, scores.shape[1]), 1)
-        allowed = (key_pos <= query_pos) & (key_pos >= start)
-        scores = jnp.where(allowed, scores, very_low)
-    return scores
-
-
 def attention_kernel(
     low_ref, full_ref, start_ref, qkv_ref, dctx_ref, out_ref,
-    key_rows, value_rows, key_acc, value_acc,
+    key_rows, value_rows, key_acc, value_acc, held_scores, held_prob,
 ):
     blocks = qkv_ref.shape[2] // BLOCK
     rows_of(qkv_ref, 1, key_rows, blocks)
@@ -336,71 +339,72 @@
         start = start_ref[:, cols]
         low, full = low_ref[j], full_ref[j]
 
-        def scores_of(i, masked):
-            return scaled_scores(
-                key_rows[block_at(i), :], query_cols, i * BLOCK, j * BLOCK, start, masked
+        def over_blocks(step, state):
+            state = step(j, True, state)
+            state = lax.fori_loop(low, full, lambda i, state: step(i, True, state), state)
+            return lax.fori_loop(full, j, lambda i, state: step(i, False, state), state)
+
+        def scores_step(i, masked, run_max):
+            scores = jnp.dot(
+                key_rows[block_at(i), :], query_cols, preferred_element_type=jnp.float32
             )
-
-        scores = scores_of(j, True)
-        run_max = jnp.max(scores, axis=0, keepdims=True)
-        prob = jnp.exp2(scores - run_max)
-        run_sum = jnp.sum(prob, axis=0, keepdims=True)
-        acc = jnp.dot(
-            qkv_ref[2, :, cols], prob.astype(jnp.bfloat16), preferred_element_type=jnp.float32
-        )
-
-        def forward(masked, i, state):
-            run_max, run_sum, acc = state
-            scores = scores_of(i, masked)
-            new_max = jnp.maximum(run_max, jnp.max(scores, axis=0, keepdims=True))
-            factor = jnp.exp2(run_max - new_max)
-            prob = jnp.exp2(scores - new_max)
-            run_sum = run_sum * factor + jnp.sum(prob, axis=0, keepdims=True)
-            acc = acc * factor + jnp.dot(
-                qkv_ref[2, :, block_at(i)],
-                prob.astype(jnp.bfloat16),
-                preferred_element_type=jnp.float32,
+            if masked:
+                key_pos = i * BLOCK + lax.broadcasted_iota(jnp.int32, scores.shape, 0)
+                query_pos = j * BLOCK + lax.broadcasted_iota(jnp.int32, (1, BLOCK), 1)
+                allowed = (key_pos <= query_pos) & (key_pos >= start)
+                scores = jnp.where(allowed, scores, very_low)
+            held_scores[i - low] = scores
+            return jnp.maximum(run_max, jnp.max(scores, axis=0, keepdims=True))
+
+        row_max = over_blocks(scores_step, jnp.full((1, BLOCK), very_low, jnp.float32))
+        shift = row_max * EXP2_SCALE
+
+        def context_step(i, state):
+            run_sum, acc = state
+            prob = jnp.exp2(held_scores[i - low] * EXP2_SCALE - shift)
+            run_sum = run_sum + jnp.sum(prob, axis=0, keepdims=True)
+            prob = prob.astype(jnp.bfloat16)
+            held_prob[i - low] = prob
+            acc = acc + jnp.dot(
+                qkv_ref[2, :, block_at(i)], prob, preferred_element_type=jnp.float32
             )
-            return new_max, run_sum, acc
-
-        state = (run_max, run_sum, acc)
-        state = lax.fori_loop(low, full, functools.partial(forward, True), state)
-        state = lax.fori_loop(full, j, functools.partial(forward, False), state)
-        run_max, run_sum, acc = state
-        context = (acc / run_sum).astype(jnp.bfloat16)
+            return run_sum, acc
+
+        run_sum, acc = lax.fori_loop(
+            low,
+            j + 1,
+            context_step,
+            (jnp.zeros((1, BLOCK), jnp.float32), jnp.zeros((HD, BLOCK), jnp.float32)),
+        )
+        inverse = 1.0 / run_sum
+        context = (acc * inverse).astype(jnp.bfloat16)
         out_ref[3, :, cols] = context
-        total = run_max + jnp.log(run_sum) * LOG2E
-        grad_cols = dctx_ref[0, :, cols]
+        grad_cols = (dctx_ref[0, :, cols].astype(jnp.float32) * inverse).astype(jnp.bfloat16)
         delta = jnp.sum(
             grad_cols.astype(jnp.float32) * context.astype(jnp.float32), axis=0, keepdims=True
         )
 
-        def backward(i, masked):
+        def grads_step(i, query_acc):
             keys = block_at(i)
-            prob = jnp.exp2(scores_of(i, masked) - total)
+            prob = held_prob[i - low]
             grad_prob = jnp.dot(
                 value_rows[keys, :], grad_cols, preferred_element_type=jnp.float32
             )
-            grad_score = (prob * (grad_prob - delta)).astype(jnp.bfloat16)
-            value_term = nt_dot(grad_cols, prob.astype(jnp.bfloat16))
-            key_term = nt_dot(query_cols, grad_score)
-            query_term = jnp.dot(
+            grad_score = (prob.astype(jnp.float32) * (grad_prob - delta)).astype(jnp.bfloat16)
+            value_acc[:, keys] += nt_dot(grad_cols, prob)
+            key_acc[:, keys] += nt_dot(query_cols, grad_score)
+            return query_acc + jnp.dot(
                 qkv_ref[1, :, keys], grad_score, preferred_element_type=jnp.float32
             )
-            return keys, key_term, value_term, query_term
-
-        keys, key_term, value_term, query_acc = backward(j, True)
-        key_acc[:, keys] = key_term
-        value_acc[:, keys] = value_term
-
-        def step(masked, i, query_acc):
-            keys, key_term, value_term, query_term = backward(i, masked)
-            key_acc[:, keys] += key_term
-            value_acc[:, keys] += value_term
-            return query_acc + query_term
-
-        query_acc = lax.fori_loop(low, full, functools.partial(step, True), query_acc)
-        query_acc = lax.fori_loop(full, j, functools.partial(step, False), query_acc)
+
+        key_acc[:, cols] = jnp.zeros((HD, BLOCK), jnp.float32)
+        value_acc[:, cols] = jnp.zeros((HD, BLOCK), jnp.float32)
+        query_acc = lax.fori_loop(
+            low,
+            j + 1,
+            grads_step,
+            jnp.zeros((HD, BLOCK), jnp.float32),
+        )
         out_ref[0, :, cols] = (query_acc * score_scale).astype(jnp.bfloat16)
         return 0
 
@@ -417,13 +421,18 @@
 
 def attention(low, full, start, qkv, dctx):
     tokens = qkv.shape[2]
+    reach = min(MAX_DOC // BLOCK + 1, tokens // BLOCK)
     return pl.pallas_call(
         attention_kernel,
         out_shape=jax.ShapeDtypeStruct((4, HD, tokens), jnp.bfloat16),
         in_specs=[SMEM, SMEM, VMEM, VMEM, VMEM],
         out_specs=VMEM,
         scratch_shapes=[pltpu.VMEM((tokens, HD), jnp.bfloat16)] * 2
-        + [pltpu.VMEM((HD, tokens), jnp.float32)] * 2,
+        + [pltpu.VMEM((HD, tokens), jnp.float32)] * 2
+        + [
+            pltpu.VMEM((reach, BLOCK, BLOCK), jnp.float32),
+            pltpu.VMEM((reach, BLOCK, BLOCK), jnp.bfloat16),
+        ],
         compiler_params=pltpu.CompilerParams(vmem_limit_bytes=40 << 20),
     )(low, full, start, qkv, dctx)
 

time: 181 us -> 161 us (0.89)
  the two profiles are of different devices: /device:TPU:0 before, /device:TPU:27 now
where the time goes in v2:
time: 161 us; the launch traced here: 163 us
  Pallas kernels  151 us (94%)
  local copies, waits for them, and re-layouts  10.7 us (7%)
    pallas_call x1, Pallas kernels, give_back(): pl.pallas_call(functools.partial(return_kernel, count), out_shape=[jax.Sh...  70.4 us
    pallas_call x1, Pallas kernels, gather(): pl.pallas_call(functools.partial(gather_kernel, count, heads), out_shape=...  49.1 us
    pallas_call x1, Pallas kernels, attention(): pl.pallas_call(attention_kernel, out_shape=jax.ShapeDtypeStruct((4, HD, t...  31.5 us
    unnamed x19, local copies, waits for them, and re-layouts  10.6 us

profile of v2, /device:TPU:27, one launch (start us, length us, event | category | flops | bytes accessed | tf_op | source)
XLA Modules:
  0.0 163.1 jit_solution(12619004239674880107)
XLA Ops:
  0.6 0.0 copy-start.5
  0.6 1.3 copy.28
  2.0 1.3 copy.29
  3.2 0.0 copy-done.5
  3.2 0.2 copy.30
  3.4 0.0 copy-start
  3.5 0.0 copy-start.3
  3.5 0.0 copy-start.4
  3.5 0.2 pad_maximum_fusion.x_ref
  3.7 1.4 copy-done
  5.0 0.1 copy-done.3
  5.1 0.0 copy-done.4
  5.1 49.1 %shard_map.93 = (bf16[3,64,4096]{2,1,0:T(8,128)(2,1)S(1)}, s32[8,4,128]{2,1,0:T(4,128)S(1)}, bf16[1,64,4096]{2,1,0:T(8,128)(2,1)S(1)}, bf16[4,512,512]{2,1,0:T(8,128)(2,1)S(1)}) custom-call(bf16[3,512,512]{2,1,0:T(8,128)(2,1)S(1)} %pad_maximum_fusion.x_ref, s32[4,128]{1,0:T(4,128)S(1)} %bitcast.27, bf16[512,512]{1,0:T(8,128)(2,1)S(1)} %copy-done.3, ...), custom_call_target="tpu_custom_call" | custom-call | tf_op jit(solution)/shard_map/pallas_call | solution.py:171
  54.2 0.0 copy-start.1
  54.2 1.1 copy-done.1
  55.4 0.1 convert_reduce_fusion
  55.5 0.1 select_reduce_fusion
  55.7 0.2 fusion
  55.9 0.0 copy-start.2
  55.9 1.4 copy-done.2
  57.3 31.5 %shard_map.94.x_ref = bf16[4,64,4096]{2,1,0:T(8,128)(2,1)S(1)} custom-call(s32[8]{0:T(128)S(1)} %get-tuple-element.37.low_ref, s32[8]{0:T(128)S(1)} %get-tuple-element.38.full_ref, s32[1,4096]{1,0:T(1,128)S(1)} %bitcast.24, bf16[3,64,4096]{2,1,0:T(8,128)(2,1)S(1)} %copy-done.2, bf16[1,64,4096]{2,1,0:T(8,128)(2,1)S(1)} %get-tuple-element.12.dctx_ref), custom_call_target="tpu_custom_call" | custom-call | tf_op jit(solution)/shard_map/pallas_call | solution.py:425
  88.8 70.4 %shard_map.95 = (bf16[3,512,512]{2,1,0:T(8,128)(2,1)S(1)}, f32[512,256]{1,0:T(8,128)S(1)}) custom-call(bf16[4,64,4096]{2,1,0:T(8,128)(2,1)S(1)} %shard_map.94.x_ref, bf16[4,512,512]{2,1,0:T(8,128)(2,1)S(1)} %get-tuple-element.13.full_ref), custom_call_target="tpu_custom_call" | custom-call | tf_op jit(solution)/shard_map/pallas_call | solution.py:282
  159.2 0.1 slice_bitcast_fusion
  159.3 1.0 copy.33
  160.3 1.0 copy.32
  161.3 1.0 copy.31
  162.3 0.8 copy.35
  (2 shorter events, 0.0 us)
Async XLA Ops:
  0.6 2.6 %copy-start.5 = (bf16[512,512]{1,0:T(8,128)(2,1)S(1)}, bf16[512,512]{1,0:T(8,128)(2,1)}, u32[]{:S(2)}) copy-start(bf16[512,512]{1,0:T(8,128)(2,1)} %param.8) | copy-start | bytes 1572868
  3.4 1.6 copy-start
  3.5 1.7 %copy-start.3 = (bf16[512,512]{1,0:T(8,128)(2,1)S(1)}, bf16[512,512]{1,0:T(8,128)(2,1)}, u32[]{:S(2)}) copy-start(bf16[512,512]{1,0:T(8,128)(2,1)} %grad_ref.1) | copy-start | bytes 1572868
  3.5 1.7 %copy-start.4 = (s32[512]{0:T(512)S(1)}, s32[512]{0:T(512)}, u32[]{:S(2)}) copy-start(s32[512]{0:T(512)} %param.9) | copy-start | bytes 6148
  54.2 1.2 copy-start.1
  55.9 1.4 copy-start.2

commit v3 on v2

--- a/solution.py
+++ b/solution.py
@@ -122,7 +122,8 @@
         remote(grad_ref, grads.at[mine], gsend, grecv, 0, "heads", far),
         remote(grad_ref, grads.at[mine], gsend, grecv, 1, "heads", sibling),
     ]
-    peers = [mod(me + step, count) for step in range(1, count)]
+    steps = sorted(range(1, count), key=lambda step: abs(step - count // 2))
+    peers = [mod(me + step, count) for step in steps]
     rest = [
         remote(doc_ref, all_doc_ref.at[me], dsend, drecv, step, "seq", peer)
         for step, peer in enumerate(peers)
@@ -210,7 +211,8 @@
     own_back = pltpu.make_async_copy(
         x_ref.at[0:3, :, token_cols(me, cols)], back_ref.at[:, here, :], local.at[1]
     )
-    peers = [mod(me + step, count) for step in range(1, count)]
+    steps = sorted(range(1, count), key=lambda step: abs(step - count // 2))
+    peers = [mod(me + step, count) for step in steps]
     first = [
         remote(x_ref.at[3, :, token_cols(peer, cols)], ctx.at[here, :], ksend, krecv, step, "seq", peer)
         for step, peer in enumerate(peers)
@@ -325,6 +327,16 @@
     lax.fori_loop(0, blocks, step, 0)
 
 
+def in_pairs(low, high, step, state):
+    pairs = lax.div(high - low, jnp.int32(2))
+    middle = low + 2 * pairs
+
+    def two(t, state):
+        return step(low + 2 * t + 1, step(low + 2 * t, state))
+
+    return lax.fori_loop(middle, high, step, lax.fori_loop(0, pairs, two, state))
+
+
 def attention_kernel(
     low_ref, full_ref, start_ref, qkv_ref, dctx_ref, out_ref,
     key_rows, value_rows, key_acc, value_acc, held_scores, held_prob,
@@ -370,7 +382,7 @@
             )
             return run_sum, acc
 
-        run_sum, acc = lax.fori_loop(
+        run_sum, acc = in_pairs(
             low,
             j + 1,
             context_step,
@@ -399,7 +411,7 @@
 
         key_acc[:, cols] = jnp.zeros((HD, BLOCK), jnp.float32)
         value_acc[:, cols] = jnp.zeros((HD, BLOCK), jnp.float32)
-        query_acc = lax.fori_loop(
+        query_acc = in_pairs(
             low,
             j + 1,
             grads_step,

time: 161 us -> 152 us (0.944)
  the two profiles are of different devices: /device:TPU:27 before, /device:TPU:0 now
where the time goes in v3:
time: 152 us; the launch traced here: 151 us
  Pallas kernels  139 us (91%)
  local copies, waits for them, and re-layouts  10.7 us (7%)
    pallas_call x1, Pallas kernels, give_back(): pl.pallas_call(functools.partial(return_kernel, count), out_shape=[jax.Sh...  64.7 us
    pallas_call x1, Pallas kernels, gather(): pl.pallas_call(functools.partial(gather_kernel, count, heads), out_shape=...  51.2 us
    pallas_call x1, Pallas kernels, attention(): pl.pallas_call(attention_kernel, out_shape=jax.ShapeDtypeStruct((4, HD, t...  22.9 us
    unnamed x19, local copies, waits for them, and re-layouts  10.6 us

profile of v3, /device:TPU:0, one launch (start us, length us, event | category | flops | bytes accessed | tf_op | source)
XLA Modules:
  0.0 150.8 jit_solution(8512224565438748569)
XLA Ops:
  0.6 0.0 copy-start.5
  0.6 1.3 copy.28
  2.0 1.3 copy.29
  3.2 0.0 copy-done.5
  3.2 0.2 copy.30
  3.4 0.0 copy-start
  3.5 0.0 copy-start.3
  3.5 0.0 copy-start.4
  3.5 0.2 pad_maximum_fusion.x_ref
  3.7 1.4 copy-done
  5.0 0.1 copy-done.3
  5.1 0.0 copy-done.4
  5.1 51.2 %shard_map.93 = (bf16[3,64,4096]{2,1,0:T(8,128)(2,1)S(1)}, s32[8,4,128]{2,1,0:T(4,128)S(1)}, bf16[1,64,4096]{2,1,0:T(8,128)(2,1)S(1)}, bf16[4,512,512]{2,1,0:T(8,128)(2,1)S(1)}) custom-call(bf16[3,512,512]{2,1,0:T(8,128)(2,1)S(1)} %pad_maximum_fusion.x_ref, s32[4,128]{1,0:T(4,128)S(1)} %bitcast.27, bf16[512,512]{1,0:T(8,128)(2,1)S(1)} %copy-done.3, ...), custom_call_target="tpu_custom_call" | custom-call | tf_op jit(solution)/shard_map/pallas_call | solution.py:172
  56.3 0.0 copy-start.1
  56.3 1.1 copy-done.1
  57.4 0.1 convert_reduce_fusion
  57.6 0.1 select_reduce_fusion
  57.7 0.2 fusion
  57.9 0.0 copy-start.2
  57.9 1.4 copy-done.2
  59.3 22.9 %shard_map.94.x_ref = bf16[4,64,4096]{2,1,0:T(8,128)(2,1)S(1)} custom-call(s32[8]{0:T(128)S(1)} %get-tuple-element.37.low_ref, s32[8]{0:T(128)S(1)} %get-tuple-element.38.full_ref, s32[1,4096]{1,0:T(1,128)S(1)} %bitcast.24, bf16[3,64,4096]{2,1,0:T(8,128)(2,1)S(1)} %copy-done.2, bf16[1,64,4096]{2,1,0:T(8,128)(2,1)S(1)} %get-tuple-element.12.dctx_ref), custom_call_target="tpu_custom_call" | custom-call | tf_op jit(solution)/shard_map/pallas_call | solution.py:437
  82.2 64.7 %shard_map.95 = (bf16[3,512,512]{2,1,0:T(8,128)(2,1)S(1)}, f32[512,256]{1,0:T(8,128)S(1)}) custom-call(bf16[4,64,4096]{2,1,0:T(8,128)(2,1)S(1)} %shard_map.94.x_ref, bf16[4,512,512]{2,1,0:T(8,128)(2,1)S(1)} %get-tuple-element.13.full_ref), custom_call_target="tpu_custom_call" | custom-call | tf_op jit(solution)/shard_map/pallas_call | solution.py:284
  146.9 0.1 slice_bitcast_fusion
  147.0 1.0 copy.33
  148.0 1.0 copy.32
  149.0 1.0 copy.31
  150.0 0.8 copy.35
  (2 shorter events, 0.0 us)
Async XLA Ops:
  0.6 2.6 %copy-start.5 = (bf16[512,512]{1,0:T(8,128)(2,1)S(1)}, bf16[512,512]{1,0:T(8,128)(2,1)}, u32[]{:S(2)}) copy-start(bf16[512,512]{1,0:T(8,128)(2,1)} %param.8) | copy-start | bytes 1572868
  3.4 1.6 %copy-start = (bf16[512,2048]{1,0:T(8,128)(2,1)S(1)}, bf16[512,2048]{1,0:T(8,128)(2,1)}, u32[]{:S(2)}) copy-start(bf16[512,2048]{1,0:T(8,128)(2,1)} %weight_ref.1) | copy-start | bytes 6291460
  3.5 1.7 %copy-start.3 = (bf16[512,512]{1,0:T(8,128)(2,1)S(1)}, bf16[512,512]{1,0:T(8,128)(2,1)}, u32[]{:S(2)}) copy-start(bf16[512,512]{1,0:T(8,128)(2,1)} %grad_ref.1) | copy-start | bytes 1572868
  3.5 1.7 %copy-start.4 = (s32[512]{0:T(512)S(1)}, s32[512]{0:T(512)}, u32[]{:S(2)}) copy-start(s32[512]{0:T(512)} %param.9) | copy-start | bytes 6148
  56.3 1.2 copy-start.1
  57.9 1.4 copy-start.2
